TPU v7x, 32 devices: a whole 2x2x4 slice. The times are simulated.
32 devices in a mesh: dp: 2 (over y), tm: 4 (over x, core), height: 4 (over z).
Axes of the slice: x: 2, y: 2, z: 4, core: 2. Of those that a mesh axis runs over, the one named last changes fastest.
Arguments:
- queries: bfloat16 [2, 16, 16, 8, 2560], P('dp', 'tm', 'height'), may hold values from -9 to 9
- keys: bfloat16 [2, 16, 16, 8, 2560], P('dp', 'tm', 'height'), may hold values from -9 to 9
- values: bfloat16 [2, 16, 16, 8, 2560], P('dp', 'tm', 'height'), may hold values from -6 to 6
- projection: bfloat16 [2560, 2560], P('dp'), may hold values from -0.125 to 0.125
- d_outputs: bfloat16 [2, 16, 16, 8, 2560], P('dp', 'tm', 'height'), may hold values from -6 to 6
Outputs:
- outputs: bfloat16 [2, 16, 16, 8, 2560], P('dp', 'tm', 'height')
- d_queries: bfloat16 [2, 16, 16, 8, 2560], P('dp', 'tm', 'height')
- d_keys: bfloat16 [2, 16, 16, 8, 2560], P('dp', 'tm', 'height')
- d_values: bfloat16 [2, 16, 16, 8, 2560], P('dp', 'tm', 'height')
All inputs are finite; a program needn't handle non-finite values.
Results may differ from a plain program's by a relative error of at most 0.01.
Values may be sent and summed in bfloat16 or wider, within the bound.
A program may use at most 128 MiB of HBM per device.

v0:
```python
import math

import jax
import jax.numpy as jnp
from jax import lax
from jax.sharding import PartitionSpec as P

HEADS = 20
HDIM = 128
TWIDE = 4
TILES_W = 2


head_groups = 4


def extended_2(cells, sides, width):
    for axis, dim in sides:
        count = lax.axis_size(axis)
        ends = count - 1
        head = lax.slice_in_dim(cells, 0, width, axis=dim)
        tail = lax.slice_in_dim(cells, cells.shape[dim] - width, cells.shape[dim], axis=dim)
        cells = jnp.concatenate(
            [
                lax.ppermute(tail, axis, [(i, (i + 1) % count) for i in range(ends)]),
                cells,
                lax.ppermute(head, axis, [((i + 1) % count, i) for i in range(ends)]),
            ],
            axis=dim,
        )
    return cells


def window_mask(
    frame_block, row_block, frame_blocks, row_blocks, tiles_across, tile_len, tile_cols
):
    grid_shape = (2, 2, tiles_across, 4, 4, tiles_across)
    query_frame = lax.broadcasted_iota(jnp.int32, grid_shape, 0)
    query_row = lax.broadcasted_iota(jnp.int32, grid_shape, 1)
    query_column = lax.broadcasted_iota(jnp.int32, grid_shape, 2)
    key_frame = lax.broadcasted_iota(jnp.int32, grid_shape, 3)
    key_row = lax.broadcasted_iota(jnp.int32, grid_shape, 4)
    key_column = lax.broadcasted_iota(jnp.int32, grid_shape, 5)
    frame_step = key_frame - query_frame - 1
    row_step = key_row - query_row - 1
    column_step = key_column - query_column
    frame_tile = 2 * frame_block + key_frame - 1
    row_tile = 2 * row_block + key_row - 1
    inside = (jnp.abs(frame_step) <= 1) & (jnp.abs(row_step) <= 1) & (jnp.abs(column_step) <= 1)
    inside = inside & (frame_tile >= 0) & (frame_tile < 2 * frame_blocks)
    inside = inside & (row_tile >= 0) & (row_tile < 2 * row_blocks)
    spread = inside[:, None, :, None, :, None, :, None, :, None, :, None]
    spread = jnp.broadcast_to(
        spread,
        (
            2,
            tile_len,
            2,
            tile_len,
            tiles_across,
            tile_cols,
            4,
            tile_len,
            4,
            tile_len,
            tiles_across,
            tile_cols,
        ),
    )
    query_count = 4 * tile_len * tile_len * tiles_across * tile_cols
    return spread.reshape(query_count, 4 * query_count)


def split_heads(matrix, group_index, group_width, head_count):
    piece = lax.dynamic_slice_in_dim(matrix, group_index * group_width, group_width, 1)
    return piece.reshape(matrix.shape[0], head_count, group_width // head_count)


def join_groups(stacked):
    return jnp.transpose(stacked, (1, 0, 2)).reshape(
        stacked.shape[1], stacked.shape[0] * stacked.shape[2]
    )


def body(queries, keys, values, projection, d_outputs):
    full_weight = lax.all_gather(projection, "dp", axis=0, tiled=True)
    tile_len = queries.shape[1] // 2
    key_value = jnp.stack((keys[0], values[0]))
    extended = extended_2(key_value, (("tm", 1), ("height", 2)), tile_len)
    query_count = queries.shape[1] * queries.shape[2] * queries.shape[3]
    model_dim = queries.shape[4]
    key_count = 4 * query_count
    query_flat = queries.reshape(query_count, model_dim)
    key_flat = extended[0].reshape(key_count, model_dim)
    value_flat = extended[1].reshape(key_count, model_dim)
    window = window_mask(
        lax.axis_index("tm"),
        lax.axis_index("height"),
        lax.axis_size("tm"),
        lax.axis_size("height"),
        TILES_W,
        tile_len,
        TWIDE,
    )
    group_width = model_dim // head_groups
    group_heads = HEADS // head_groups
    scaling = 1.0 / math.sqrt(HDIM)

    def forward_group(group_index):
        query_heads = split_heads(query_flat, group_index, group_width, group_heads)
        key_heads = split_heads(key_flat, group_index, group_width, group_heads)
        value_heads = split_heads(value_flat, group_index, group_width, group_heads)
        scores = (
            jnp.einsum("qhd,khd->hqk", query_heads, key_heads, preferred_element_type=jnp.float32)
            * scaling
        )
        masked = jnp.where(window[None], scores, -jnp.inf)
        largest = jnp.max(masked, axis=2, keepdims=True)
        weights = jnp.exp(masked - largest)
        soft_weights = (weights / jnp.sum(weights, axis=2, keepdims=True)).astype(jnp.bfloat16)
        attended = jnp.einsum(
            "hqk,khd->qhd", soft_weights, value_heads, preferred_element_type=jnp.float32
        )
        return (attended.reshape(query_count, group_width).astype(jnp.bfloat16), soft_weights)

    group_ids = jnp.arange(head_groups, dtype=jnp.int32)
    attended_groups, weight_groups = lax.map(forward_group, group_ids)
    attended = join_groups(attended_groups)
    outputs = jnp.dot(attended, full_weight, preferred_element_type=jnp.float32).astype(
        jnp.bfloat16
    )
    cotangent = d_outputs.reshape(query_count, d_outputs.shape[4])
    grad_attended = lax.dot_general(
        cotangent, full_weight, (((1,), (1,)), ((), ())), preferred_element_type=jnp.float32
    ).astype(jnp.bfloat16)

    def backward_group(group_items):
        group_index, soft_weights = group_items
        query_heads = split_heads(query_flat, group_index, group_width, group_heads)
        key_heads = split_heads(key_flat, group_index, group_width, group_heads)
        value_heads = split_heads(value_flat, group_index, group_width, group_heads)
        grad_heads = split_heads(grad_attended, group_index, group_width, group_heads)
        weights_wide = soft_weights.astype(jnp.float32)
        grad_weights = jnp.einsum(
            "qhd,khd->hqk", grad_heads, value_heads, preferred_element_type=jnp.float32
        )
        row_dot = jnp.sum(weights_wide * grad_weights, axis=2, keepdims=True)
        grad_scores = (weights_wide * (grad_weights - row_dot) * scaling).astype(jnp.bfloat16)
        grad_query = jnp.einsum(
            "hqk,khd->qhd", grad_scores, key_heads, preferred_element_type=jnp.float32
        )
        grad_key = jnp.einsum(
            "hqk,qhd->khd", grad_scores, query_heads, preferred_element_type=jnp.float32
        )
        grad_value = jnp.einsum(
            "hqk,qhd->khd", soft_weights, grad_heads, preferred_element_type=jnp.float32
        )
        return (
            grad_query.reshape(query_count, group_width).astype(jnp.bfloat16),
            grad_key.reshape(key_count, group_width),
            grad_value.reshape(key_count, group_width),
        )

    query_groups, key_groups, value_groups = lax.map(backward_group, (group_ids, weight_groups))
    key_grads = join_groups(key_groups).reshape(extended.shape[1:])
    value_grads = join_groups(value_groups).reshape(extended.shape[1:])
    grads_ext = jnp.stack((key_grads, value_grads))
    low_rim = grads_ext[:, :tile_len].astype(jnp.bfloat16)
    high_rim = grads_ext[:, 3 * tile_len :].astype(jnp.bfloat16)
    outgoing = jnp.concatenate((low_rim, high_rim), axis=1)
    arrived = extended_2(outgoing, (("tm", 1),), tile_len)
    incoming = jnp.concatenate((arrived[:, :tile_len], arrived[:, 3 * tile_len :]), axis=1)
    middle = grads_ext[:, tile_len : 3 * tile_len]
    own_rims = jnp.concatenate(
        (middle[:, :, :tile_len], middle[:, :, 3 * tile_len :]), axis=2
    ).astype(jnp.bfloat16)
    corner_rims = jnp.concatenate(
        (incoming[:, :, :tile_len], incoming[:, :, 3 * tile_len :]), axis=2
    )
    row_parcel = jnp.stack((own_rims, corner_rims))
    row_arrived = extended_2(row_parcel, (("height", 3),), tile_len)
    from_rows = jnp.concatenate(
        (row_arrived[:, :, :, :tile_len], row_arrived[:, :, :, 3 * tile_len :]), axis=3
    )
    summed = middle[:, :, tile_len : 3 * tile_len] + incoming[:, :, tile_len : 3 * tile_len].astype(
        jnp.float32
    )
    summed = summed + from_rows[0].astype(jnp.float32) + from_rows[1].astype(jnp.float32)
    summed = summed.astype(jnp.bfloat16)
    d_queries = join_groups(query_groups).reshape(queries.shape)
    return (
        outputs.reshape(d_outputs.shape),
        d_queries,
        summed[0].reshape(keys.shape),
        summed[1].reshape(values.shape),
    )


def solution(mesh):
    in_specs = (
        P("dp", "tm", "height", None, None),
        P("dp", "tm", "height", None, None),
        P("dp", "tm", "height", None, None),
        P("dp", None),
        P("dp", "tm", "height", None, None),
    )
    out_specs = (
        P("dp", "tm", "height", None, None),
        P("dp", "tm", "height", None, None),
        P("dp", "tm", "height", None, None),
        P("dp", "tm", "height", None, None),
    )
    return jax.shard_map(body, mesh=mesh, in_specs=in_specs, out_specs=out_specs, check_vma=False)
```

profile of v0, /device:TPU:1, one launch (start us, length us, event | category | flops | bytes accessed | tf_op | source)
XLA Modules:
  0.0 338.6 jit_solution(11113361549121396555)
XLA Ops:
  8.7 4.5 %collective-permute-start = (bf16[2,2,4,8,2560]{4,3,2,1,0:T(8,128)(2,1)S(1)}, bf16[2,2,4,8,2560]{4,3,2,1,0:T(8,128)(2,1)S(1)}, u32[]{:S(2)}, u32[]{:S(2)}) collective-permute-start(bf16[2,2,4,8,2560]{4,3,2,1,0:T(8,128)(2,1)S(1)} %get-tuple-element.227), channel_id=1, source_target_pairs={{0,4},{4,8},{8,12},{1,5},{5,9},{9,13},{2,6},{6,10},{10,14},{3,7},{... | collective-permute-start | bytes 1966088 | tf_op jit(solution)/shard_map/ppermute | solution.py:25
  15.1 5.6 %collective-permute-done = bf16[2,2,4,8,2560]{4,3,2,1,0:T(8,128)(2,1)S(1)} collective-permute-done((bf16[2,2,4,8,2560]{4,3,2,1,0:T(8,128)(2,1)S(1)}, bf16[2,2,4,8,2560]{4,3,2,1,0:T(8,128)(2,1)S(1)}, u32[]{:S(2)}, u32[]{:S(2)}) %collective-permute-start) | collective-permute-done | bytes 655392 | tf_op jit(solution)/shard_map/ppermute | solution.py:25
  27.2 4.6 %collective-permute-start.2 = (bf16[2,8,2,8,2560]{4,3,2,1,0:T(8,128)(2,1)}, bf16[2,8,2,8,2560]{4,3,2,1,0:T(8,128)(2,1)}, u32[]{:S(2)}, u32[]{:S(2)}) collective-permute-start(bf16[2,8,2,8,2560]{4,3,2,1,0:T(8,128)(2,1)} %get-tuple-element.223), channel_id=1, source_target_pairs={{0,1},{1,2},{2,3},{4,5},{5,6},{6,7},{8,9},{9,10},{10,11},{12,13},{... | collective-permute-start | bytes 3932168 | tf_op jit(solution)/shard_map/ppermute | solution.py:25
  35.5 16.3 %collective-permute-done.2 = bf16[2,8,2,8,2560]{4,3,2,1,0:T(8,128)(2,1)} collective-permute-done((bf16[2,8,2,8,2560]{4,3,2,1,0:T(8,128)(2,1)}, bf16[2,8,2,8,2560]{4,3,2,1,0:T(8,128)(2,1)}, u32[]{:S(2)}, u32[]{:S(2)}) %collective-permute-start.2) | collective-permute-done | bytes 1310752 | tf_op jit(solution)/shard_map/ppermute | solution.py:25
  51.8 5.4 %collective-permute-done.3 = bf16[2,8,2,8,2560]{4,3,2,1,0:T(8,128)(2,1)} collective-permute-done((bf16[2,8,2,8,2560]{4,3,2,1,0:T(8,128)(2,1)}, bf16[2,8,2,8,2560]{4,3,2,1,0:T(8,128)(2,1)}, u32[]{:S(2)}, u32[]{:S(2)}) %collective-permute-start.3) | collective-permute-done | bytes 1310752 | tf_op jit(solution)/shard_map/ppermute | solution.py:27
  70.1 95.3 %while.28 = (s32[]{:T(128)}, bf16[4,128,640]{1,2,0:T(8,128)(2,1)}, bf16[4,5,128,512]{3,2,1,0:T(8,128)(2,1)}, s32[4]{0:T(128)S(1)}, bf16[512,2560]{0,1:T(8,128)(2...) while((s32[]{:T(128)}, bf16[4,128,640]{1,2,0:T(8,128)(2,1)}, ...), condition=%wide.region_3.4_spmd.clone, body=%wide.region_0.3_spmd.clone.sunk | while | flops 170476032 | bytes 9772999 | solution.py:127
  73.6 5.4 %broadcast_in_dim.70 = pred[2,2,2,2,2,4,4,2,4,2,2,4]{11,10,9,8,7,6,5,4,3,2,1,0:T(4,128)(4,1)} broadcast(pred[2,2,2,4,4,2]{5,4,3,2,1,0:T(4,128)(4,1)S(1)} %get-tuple-element.386), dimensions={0,2,4,6,8,10} | broadcast | bytes 65792 | tf_op jit(solution)/shard_map/broadcast_in_dim | solution.py:53
  79.0 12.1 %broadcast_in_dim.71 = pred[128,512]{1,0:T(8,128)(4,1)S(1)} reshape(pred[2,2,2,2,2,4,4,2,4,2,2,4]{11,10,9,8,7,6,5,4,3,2,1,0:T(4,128)(4,1)} %broadcast_in_dim.70) | data formatting | bytes 131072 | tf_op jit(solution)/shard_map/while/body/eval_jaxpr/jit(_where)/broadcast_in_dim | solution.py:117
  97.5 5.4 %broadcast_in_dim.70 = pred[2,2,2,2,2,4,4,2,4,2,2,4]{11,10,9,8,7,6,5,4,3,2,1,0:T(4,128)(4,1)} broadcast(pred[2,2,2,4,4,2]{5,4,3,2,1,0:T(4,128)(4,1)S(1)} %get-tuple-element.386), dimensions={0,2,4,6,8,10} | broadcast | bytes 65792 | tf_op jit(solution)/shard_map/broadcast_in_dim | solution.py:53
  102.8 12.1 %broadcast_in_dim.71 = pred[128,512]{1,0:T(8,128)(4,1)S(1)} reshape(pred[2,2,2,2,2,4,4,2,4,2,2,4]{11,10,9,8,7,6,5,4,3,2,1,0:T(4,128)(4,1)} %broadcast_in_dim.70) | data formatting | bytes 131072 | tf_op jit(solution)/shard_map/while/body/eval_jaxpr/jit(_where)/broadcast_in_dim | solution.py:117
  121.3 5.4 %broadcast_in_dim.70 = pred[2,2,2,2,2,4,4,2,4,2,2,4]{11,10,9,8,7,6,5,4,3,2,1,0:T(4,128)(4,1)} broadcast(pred[2,2,2,4,4,2]{5,4,3,2,1,0:T(4,128)(4,1)S(1)} %get-tuple-element.386), dimensions={0,2,4,6,8,10} | broadcast | bytes 65792 | tf_op jit(solution)/shard_map/broadcast_in_dim | solution.py:53
  126.7 12.1 %broadcast_in_dim.71 = pred[128,512]{1,0:T(8,128)(4,1)S(1)} reshape(pred[2,2,2,2,2,4,4,2,4,2,2,4]{11,10,9,8,7,6,5,4,3,2,1,0:T(4,128)(4,1)} %broadcast_in_dim.70) | data formatting | bytes 131072 | tf_op jit(solution)/shard_map/while/body/eval_jaxpr/jit(_where)/broadcast_in_dim | solution.py:117
  145.1 5.4 %broadcast_in_dim.70 = pred[2,2,2,2,2,4,4,2,4,2,2,4]{11,10,9,8,7,6,5,4,3,2,1,0:T(4,128)(4,1)} broadcast(pred[2,2,2,4,4,2]{5,4,3,2,1,0:T(4,128)(4,1)S(1)} %get-tuple-element.386), dimensions={0,2,4,6,8,10} | broadcast | bytes 65792 | tf_op jit(solution)/shard_map/broadcast_in_dim | solution.py:53
  150.5 12.1 %broadcast_in_dim.71 = pred[128,512]{1,0:T(8,128)(4,1)S(1)} reshape(pred[2,2,2,2,2,4,4,2,4,2,2,4]{11,10,9,8,7,6,5,4,3,2,1,0:T(4,128)(4,1)} %broadcast_in_dim.70) | data formatting | bytes 131072 | tf_op jit(solution)/shard_map/while/body/eval_jaxpr/jit(_where)/broadcast_in_dim | solution.py:117
  165.4 4.6 %all-gather.2.cloned.1.call-done = bf16[2560,2560]{1,0:T(8,128)(2,1)} async-done(((bf16[1280,2560]{1,0:T(8,128)(2,1)}), bf16[2560,2560]{1,0:T(8,128)(2,1)}) %all-gather.2.cloned.1.call-update) | async-done | bytes 13107216 | tf_op jit(solution)/shard_map/all_gather | solution.py:86
  170.0 9.8 %convolution_convert_fusion.2 = bf16[128,2560]{1,0:T(8,128)(2,1)} fusion(bf16[128,2560]{1,0:T(8,128)(2,1)S(1)} %bitcast.136, bf16[2560,2560]{1,0:T(8,128)(2,1)} %all-gather.2.cloned.1.call-done), kind=kOutput, calls=%fused_computation.49 | convolution fusion | flops 1678049280 | bytes 14417920 | tf_op jit(solution)/shard_map/dot_general | solution.py:133
  180.7 54.4 %while.27 = (s32[]{:T(128)}, bf16[4,128,640]{1,2,0:T(8,128)(2,1)}, f32[4,512,640]{1,2,0:T(8,128)}, f32[4,512,640]{1,2,0:T(8,128)}, s32[4]{0:T(128)S(1)}, /*index...) while((s32[]{:T(128)}, bf16[4,128,640]{1,2,0:T(8,128)(2,1)}, ...), condition=%wide.region_6.7_spmd, body=%wide.region_4.6_spmd.sunk | while | flops 340216064 | bytes 23595236 | solution.py:164
  235.2 7.2 %copy.43 = f32[512,4,640]{2,1,0:T(4,128)} copy(f32[512,4,640]{0,2,1:T(8,128)} %bitcast.148) | data formatting | bytes 10485760 | tf_op jit(solution)/shard_map/transpose | solution.py:80
  242.4 7.4 %stack_reshape_reshape.7 = f32[1,8,8,8,2560]{4,3,2,1,0:T(8,128)} reshape(f32[512,4,640]{2,1,0:T(4,128)} %copy.43) | data formatting | bytes 10485760 | tf_op jit(solution)/shard_map/stack;reshape;reshape | solution.py:167
  249.8 7.2 %copy.42 = f32[512,4,640]{2,1,0:T(4,128)} copy(f32[512,4,640]{0,2,1:T(8,128)} %bitcast.149) | data formatting | bytes 10485760 | tf_op jit(solution)/shard_map/transpose | solution.py:80
  257.1 7.5 %stack_reshape_reshape.6 = f32[1,8,8,8,2560]{4,3,2,1,0:T(8,128)} reshape(f32[512,4,640]{2,1,0:T(4,128)} %copy.42) | data formatting | bytes 10485760 | tf_op jit(solution)/shard_map/stack;reshape;reshape | solution.py:167
  285.0 11.2 %collective-permute-done.4 = bf16[2,2,8,8,2560]{4,3,2,1,0:T(8,128)(2,1)S(1)} collective-permute-done((bf16[2,2,8,8,2560]{4,3,2,1,0:T(8,128)(2,1)S(1)}, bf16[2,2,8,8,2560]{4,3,2,1,0:T(8,128)(2,1)S(1)}, u32[]{:S(2)}, u32[]{:S(2)}) %collective-permute-start.4) | collective-permute-done | bytes 1310752 | tf_op jit(solution)/shard_map/ppermute | solution.py:25
  296.3 4.7 %collective-permute-done.5 = bf16[2,2,8,8,2560]{4,3,2,1,0:T(8,128)(2,1)S(1)} collective-permute-done((bf16[2,2,8,8,2560]{4,3,2,1,0:T(8,128)(2,1)S(1)}, bf16[2,2,8,8,2560]{4,3,2,1,0:T(8,128)(2,1)S(1)}, u32[]{:S(2)}, u32[]{:S(2)}) %collective-permute-start.5) | collective-permute-done | bytes 1310752 | tf_op jit(solution)/shard_map/ppermute | solution.py:27
  313.3 7.5 %convolution_convert_fusion.3 = bf16[128,2560]{1,0:T(8,128)(2,1)} fusion(bf16[128,2560]{0,1:T(8,128)(2,1)S(1)} %bitcast.153, bf16[2560,2560]{1,0:T(8,128)(2,1)} %all-gather.2.cloned.1.call-done), kind=kOutput, calls=%fused_computation.50 | convolution fusion | flops 1678049280 | bytes 14417920 | tf_op jit(solution)/shard_map/dot_general | solution.py:129
  (136 shorter events, 145.3 us)
Async XLA Ops:
  7.2 162.8 %copy-start = (bf16[1,4,4,8,2560]{4,3,2,1,0:T(8,128)(2,1)S(1)}, bf16[1,4,4,8,2560]{4,3,2,1,0:T(8,128)(2,1)}, u32[]{:S(2)}) copy-start(bf16[1,4,4,8,2560]{4,3,2,1,0:T(8,128)(2,1)} %param.13) | copy-start | bytes 1966084
  7.2 1.2 copy-start.4
  7.2 1.3 copy-start.5
  7.2 162.8 %all-gather.2.cloned.1.call-start = ((), (), s32[]{:S(2)}) async-start(), calls=%async_computation | async-start | bytes 19660800 | tf_op jit(solution)/shard_map/all_gather | solution.py:86
  8.7 12.0 %collective-permute-start = (bf16[2,2,4,8,2560]{4,3,2,1,0:T(8,128)(2,1)S(1)}, bf16[2,2,4,8,2560]{4,3,2,1,0:T(8,128)(2,1)S(1)}, u32[]{:S(2)}, u32[]{:S(2)}) collective-permute-start(bf16[2,2,4,8,2560]{4,3,2,1,0:T(8,128)(2,1)S(1)} %get-tuple-element.227), channel_id=1, source_target_pairs={{0,4},{4,8},{8,12},{1,5},{5,9},{9,13},{2,6},{6,10},{10,14},{3,7},{... | collective-permute-start | bytes 1966088 | tf_op jit(solution)/shard_map/ppermute | solution.py:25
  13.2 11.9 %collective-permute-start.1 = (bf16[2,2,4,8,2560]{4,3,2,1,0:T(8,128)(2,1)S(1)}, bf16[2,2,4,8,2560]{4,3,2,1,0:T(8,128)(2,1)S(1)}, u32[]{:S(2)}, u32[]{:S(2)}) collective-permute-start(bf16[2,2,4,8,2560]{4,3,2,1,0:T(8,128)(2,1)S(1)} %get-tuple-element.228), channel_id=1, source_target_pairs={{4,0},{8,4},{12,8},{5,1},{9,5},{13,9},{6,2},{10,6},{14,10},{7,3},{... | collective-permute-start | bytes 1966088 | tf_op jit(solution)/shard_map/ppermute | solution.py:27
  27.2 24.7 %collective-permute-start.2 = (bf16[2,8,2,8,2560]{4,3,2,1,0:T(8,128)(2,1)}, bf16[2,8,2,8,2560]{4,3,2,1,0:T(8,128)(2,1)}, u32[]{:S(2)}, u32[]{:S(2)}) collective-permute-start(bf16[2,8,2,8,2560]{4,3,2,1,0:T(8,128)(2,1)} %get-tuple-element.223), channel_id=1, source_target_pairs={{0,1},{1,2},{2,3},{4,5},{5,6},{6,7},{8,9},{9,10},{10,11},{12,13},{... | collective-permute-start | bytes 3932168 | tf_op jit(solution)/shard_map/ppermute | solution.py:25
  31.8 25.4 %collective-permute-start.3 = (bf16[2,8,2,8,2560]{4,3,2,1,0:T(8,128)(2,1)}, bf16[2,8,2,8,2560]{4,3,2,1,0:T(8,128)(2,1)}, u32[]{:S(2)}, u32[]{:S(2)}) collective-permute-start(bf16[2,8,2,8,2560]{4,3,2,1,0:T(8,128)(2,1)} %get-tuple-element.224), channel_id=1, source_target_pairs={{1,0},{2,1},{3,2},{5,4},{6,5},{7,6},{9,8},{10,9},{11,10},{13,12},{... | collective-permute-start | bytes 3932168 | tf_op jit(solution)/shard_map/ppermute | solution.py:27
  270.6 5.5 %copy-start.2 = (f32[2,8,8,8,2560]{4,3,2,1,0:T(8,128)}, f32[2,8,8,8,2560]{4,3,2,1,0:T(8,128)S(1)}, u32[]{:S(2)}) copy-start(f32[2,8,8,8,2560]{4,3,2,1,0:T(8,128)S(1)} %constant_dynamic-update-slice_fusion.6) | copy-start | bytes 31457284
  278.0 18.2 %collective-permute-start.4 = (bf16[2,2,8,8,2560]{4,3,2,1,0:T(8,128)(2,1)S(1)}, bf16[2,2,8,8,2560]{4,3,2,1,0:T(8,128)(2,1)S(1)}, u32[]{:S(2)}, u32[]{:S(2)}) collective-permute-start(bf16[2,2,8,8,2560]{4,3,2,1,0:T(8,128)(2,1)S(1)} %get-tuple-element.216), channel_id=1, source_target_pairs={{0,4},{4,8},{8,12},{1,5},{5,9},{9,13},{2,6},{6,10},{10,14},{3,7},{... | collective-permute-start | bytes 3932168 | tf_op jit(solution)/shard_map/ppermute | solution.py:25
  281.7 19.3 %collective-permute-start.5 = (bf16[2,2,8,8,2560]{4,3,2,1,0:T(8,128)(2,1)S(1)}, bf16[2,2,8,8,2560]{4,3,2,1,0:T(8,128)(2,1)S(1)}, u32[]{:S(2)}, u32[]{:S(2)}) collective-permute-start(bf16[2,2,8,8,2560]{4,3,2,1,0:T(8,128)(2,1)S(1)} %get-tuple-element.215), channel_id=1, source_target_pairs={{4,0},{8,4},{12,8},{5,1},{9,5},{13,9},{6,2},{10,6},{14,10},{7,3},{... | collective-permute-start | bytes 3932168 | tf_op jit(solution)/shard_map/ppermute | solution.py:27
  303.3 10.0 %copy-start.3 = (bf16[4,128,640]{1,2,0:T(8,128)(2,1)S(1)}, bf16[4,128,640]{1,2,0:T(8,128)(2,1)}, u32[]{:S(2)}) copy-start(bf16[4,128,640]{1,2,0:T(8,128)(2,1)} %get-tuple-element.101) | copy-start | bytes 1966084
  303.3 18.2 %collective-permute-start.6 = (bf16[2,2,4,2,8,2560]{5,4,3,2,1,0:T(8,128)(2,1)}, bf16[2,2,4,2,8,2560]{5,4,3,2,1,0:T(8,128)(2,1)}, u32[]{:S(2)}, u32[]{:S(2)}) collective-permute-start(bf16[2,2,4,2,8,2560]{5,4,3,2,1,0:T(8,128)(2,1)} %get-tuple-element.220), channel_id=1, source_target_pairs={{0,1},{1,2},{2,3},{4,5},{5,6},{6,7},{8,9},{9,10},{10,11},{12,13},{... | collective-permute-start | bytes 3932168 | tf_op jit(solution)/shard_map/ppermute | solution.py:25
  307.6 19.1 %collective-permute-start.7 = (bf16[2,2,4,2,8,2560]{5,4,3,2,1,0:T(8,128)(2,1)}, bf16[2,2,4,2,8,2560]{5,4,3,2,1,0:T(8,128)(2,1)}, u32[]{:S(2)}, u32[]{:S(2)}) collective-permute-start(bf16[2,2,4,2,8,2560]{5,4,3,2,1,0:T(8,128)(2,1)} %get-tuple-element.219), channel_id=1, source_target_pairs={{1,0},{2,1},{3,2},{5,4},{6,5},{7,6},{9,8},{10,9},{11,10},{13,12},{... | collective-permute-start | bytes 3932168 | tf_op jit(solution)/shard_map/ppermute | solution.py:27
  328.1 3.6 %copy-start.1 = (bf16[1,4,4,8,2560]{4,3,2,1,0:T(8,128)(2,1)S(1)}, bf16[1,4,4,8,2560]{4,3,2,1,0:T(8,128)(2,1)}, u32[]{:S(2)}) copy-start(bf16[1,4,4,8,2560]{4,3,2,1,0:T(8,128)(2,1)} %param.13) | copy-start | bytes 1966084
Sparse Core Ops, SparseCore 0:
  9.6 160.3 all-gather.1
where the time goes:
time: 342 us; the launch traced here: 339 us
  local copies, waits for them, and re-layouts  180 us (53%)
  waiting for transfers between devices  57.4 us (17%)
  matrix products  43.7 us (13%)
  starting transfers between devices  23.5 us (7%)
  between operations  14.3 us (4%)
  other arithmetic  13.8 us (4%)
  loops' own time  5.66 us (2%)
    broadcast_in_dim x4, local copies, waits for them, and re-layouts, forward_group(): masked = jnp.where(window[None], scores, -jnp.inf)  48.2 us
    ppermute x4, waiting for transfers between devices, extended_2(): lax.ppermute(tail, axis, [(i, (i + 1) % count) for i in range(ends)])  33.9 us
    dynamic_slice x28, local copies, waits for them, and re-layouts, split_heads(): lax.dynamic_slice_in_dim(matrix, group_index * group_width, group_width, 1)  26.5 us
    broadcast_in_dim x4, local copies, waits for them, and re-layouts, window_mask(): jnp.broadcast_to(spread, (2, tile_len, 2, tile_len, tiles_across, tile_co...  21.5 us
    ppermute x4, waiting for transfers between devices, extended_2(): lax.ppermute(head, axis, [((i + 1) % count, i) for i in range(ends)])  18.2 us
    another operation x3, local copies, waits for them, and re-layouts, body(): grads_ext = jnp.stack((key_grads, value_grads))  17.9 us
    ppermute x4, starting transfers between devices, extended_2(): lax.ppermute(tail, axis, [(i, (i + 1) % count) for i in range(ends)])  17.1 us
    transpose x3, local copies, waits for them, and re-layouts, join_groups(): jnp.transpose(stacked, (1, 0, 2))  16.6 us
  transfers between devices with their start and end apart: 9, of which 9 were waited for; matrix products, arithmetic and copies ran while one was open for 37% of the time, Pallas kernels for 0%

commit v1 on v0

v1 whole, which is shorter than its diff:
```python
import functools
import math

import jax
import jax.numpy as jnp
import numpy as np
from jax import lax
from jax.experimental import pallas as pl
from jax.experimental.pallas import tpu as pltpu
from jax.sharding import PartitionSpec as P

HEADS = 20
HDIM = 128
TWIDE = 4
TILES_W = 2

FAR = -1e30


def key_tiles():
    own, low, high = (1, 2), (0,), (3,)
    return (
        (own, own),
        (own, low),
        (own, high),
        (low, own),
        (high, own),
        (low, low),
        (low, high),
        (high, low),
        (high, high),
    )


def tile_coords(tile_len, cols):
    frames, rows = [], []
    for frame_tiles, row_tiles in key_tiles():
        f = np.repeat(np.array(frame_tiles), tile_len)
        r = np.repeat(np.array(row_tiles), tile_len)
        frames.append(np.broadcast_to(f[:, None, None], (len(f), len(r), cols)).reshape(-1))
        rows.append(np.broadcast_to(r[None, :, None], (len(f), len(r), cols)).reshape(-1))
    return np.concatenate(frames), np.concatenate(rows)


def window_bias(tile_len, cols, tile_cols):
    frames, rows = tile_coords(tile_len, cols)
    query_count = 4 * tile_len * tile_len * cols
    query_frames, query_rows = frames[:query_count], rows[:query_count]
    column_tiles = np.arange(cols) // tile_cols
    key_columns = np.tile(column_tiles, len(frames) // cols)
    query_columns = np.tile(column_tiles, query_count // cols)
    inside = np.abs(frames[:, None] - query_frames[None]) <= 1
    inside &= np.abs(rows[:, None] - query_rows[None]) <= 1
    inside &= np.abs(key_columns[:, None] - query_columns[None]) <= 1
    frame_block, frame_blocks = lax.axis_index("tm"), lax.axis_size("tm")
    row_block, row_blocks = lax.axis_index("height"), lax.axis_size("height")
    frame_tile = 2 * frame_block + jnp.asarray(frames, jnp.int32)[:, None] - 1
    row_tile = 2 * row_block + jnp.asarray(rows, jnp.int32)[:, None] - 1
    present = (frame_tile >= 0) & (frame_tile < 2 * frame_blocks)
    present = present & (row_tile >= 0) & (row_tile < 2 * row_blocks)
    return jnp.where(present & jnp.asarray(inside), 0.0, FAR).astype(jnp.float32)


def rows_of(value):
    return value.astype(jnp.float32).reshape(-1, value.shape[-1]).astype(jnp.bfloat16)


def attention_kernel(
    heads,
    scaling,
    bias_ref,
    q_ref,
    k_ref,
    v_ref,
    top_ref,
    bottom_ref,
    left_ref,
    right_ref,
    corner_left_ref,
    corner_right_ref,
    da_ref,
    att_ref,
    dq_ref,
    d_own_ref,
    d_top_ref,
    d_bottom_ref,
    d_left_ref,
    d_right_ref,
    d_corner_left_ref,
    d_corner_right_ref,
):
    f32 = jnp.float32

    def gather(which, own_ref, cols):
        parts = [rows_of(own_ref[:, :, :, cols])]
        for ref in (top_ref, bottom_ref, left_ref, right_ref):
            parts.append(rows_of(ref[which, :, :, :, cols]))
        for ref in (corner_left_ref, corner_right_ref):
            for side in range(2):
                parts.append(rows_of(ref[which, side, :, :, :, cols]))
        return jnp.concatenate(parts, axis=0)

    def scatter(which, grads, cols):
        start = 0
        for ref in (d_own_ref, d_top_ref, d_bottom_ref, d_left_ref, d_right_ref):
            shape = ref.shape[1:-1] + (HDIM,)
            count = shape[0] * shape[1] * shape[2]
            part = grads[start : start + count].reshape(shape)
            ref[which, :, :, :, cols] = part.astype(ref.dtype)
            start += count
        for ref in (d_corner_left_ref, d_corner_right_ref):
            shape = ref.shape[2:-1] + (HDIM,)
            count = shape[0] * shape[1] * shape[2]
            for side in range(2):
                part = grads[start : start + count].reshape(shape)
                ref[which, side, :, :, :, cols] = part.astype(ref.dtype)
                start += count

    for head in range(heads):
        cols = slice(head * HDIM, (head + 1) * HDIM)
        q = rows_of(q_ref[:, :, :, cols])
        k = gather(0, k_ref, cols)
        v = gather(1, v_ref, cols)
        da = da_ref[:, cols]
        scores = lax.dot_general(k, q, (((1,), (1,)), ((), ())), preferred_element_type=f32)
        scores = scores * scaling + bias_ref[...]
        largest = jnp.max(scores, axis=0, keepdims=True)
        weights = jnp.exp(scores - largest)
        inverse = 1.0 / jnp.sum(weights, axis=0, keepdims=True)
        probs = (weights * inverse).astype(jnp.bfloat16)
        att = lax.dot_general(probs, v, (((0,), (0,)), ((), ())), preferred_element_type=f32)
        att_ref[:, cols] = att.astype(att_ref.dtype)
        wide = probs.astype(f32)
        d_probs = lax.dot_general(v, da, (((1,), (1,)), ((), ())), preferred_element_type=f32)
        row_dot = jnp.sum(wide * d_probs, axis=0, keepdims=True)
        d_scores = (wide * (d_probs - row_dot) * scaling).astype(jnp.bfloat16)
        dq = lax.dot_general(d_scores, k, (((0,), (0,)), ((), ())), preferred_element_type=f32)
        shape = dq_ref.shape[:-1] + (HDIM,)
        dq_ref[:, :, :, cols] = dq.reshape(shape).astype(dq_ref.dtype)
        scatter(0, jnp.dot(d_scores, q, preferred_element_type=f32), cols)
        scatter(1, jnp.dot(probs, da, preferred_element_type=f32), cols)


def attention(bias, q, k, v, pieces, da):
    width = 2 * HDIM if HEADS % 2 == 0 else HDIM
    dim = q.shape[-1]

    def blocked(array):
        lead = array.ndim - 1
        return pl.BlockSpec(array.shape[:-1] + (width,), lambda i: (0,) * lead + (i,))

    operands = (q, k, v, *pieces, da)
    grads = [jax.ShapeDtypeStruct((2,) + k.shape, jnp.float32)]
    grads += [jax.ShapeDtypeStruct(p.shape, jnp.bfloat16) for p in pieces]
    outs = [jax.ShapeDtypeStruct(da.shape, jnp.bfloat16), jax.ShapeDtypeStruct(q.shape, q.dtype)]
    outs += grads
    keys, queries = bias.shape
    moved = 2 * sum(math.prod(a.shape) for a in operands + tuple(outs))
    return pl.pallas_call(
        functools.partial(attention_kernel, width // HDIM, 1.0 / math.sqrt(HDIM)),
        grid=(dim // width,),
        out_shape=outs,
        in_specs=[pl.BlockSpec(bias.shape, lambda i: (0, 0))] + [blocked(a) for a in operands],
        out_specs=[blocked(o) for o in outs],
        compiler_params=pltpu.CompilerParams(vmem_limit_bytes=40 * 1024 * 1024),
        cost_estimate=pl.CostEstimate(
            flops=12 * keys * queries * dim,
            bytes_accessed=moved,
            transcendentals=keys * queries * dim // HDIM,
        ),
        name="attention",
    )(bias, *operands)


def shifted(array, axis, step):
    count = lax.axis_size(axis)
    pairs = [(i, i + step) for i in range(count) if 0 <= i + step < count]
    return lax.ppermute(array, axis, pairs)


def rotated(array, axis, step):
    count = lax.axis_size(axis)
    return lax.ppermute(array, axis, [(i, (i + step) % count) for i in range(count)])


def contract(x, weight, weight_axis):
    return lax.dot_general(
        x, weight, (((1,), (weight_axis,)), ((), ())), preferred_element_type=jnp.float32
    )


def body(queries, keys, values, projection, d_outputs):
    f32, bf16 = jnp.float32, jnp.bfloat16
    q, k, v = queries[0], keys[0], values[0]
    frames, rows, cols, dim = q.shape
    tile_len = frames // 2
    query_count = frames * rows * cols
    depth = projection.shape[0]
    dp_count, dp_index = lax.axis_size("dp"), lax.axis_index("dp")

    low_rows = jnp.stack((k[:, :tile_len], v[:, :tile_len]))
    high_rows = jnp.stack((k[:, tile_len:], v[:, tile_len:]))
    low_frames = jnp.stack((k[:tile_len], v[:tile_len]))
    high_frames = jnp.stack((k[tile_len:], v[tile_len:]))
    top = shifted(high_rows, "height", 1)
    bottom = shifted(low_rows, "height", -1)
    left = shifted(high_frames, "tm", 1)
    right = shifted(low_frames, "tm", -1)
    corner_left = shifted(jnp.stack((top[:, tile_len:], bottom[:, tile_len:]), 1), "tm", 1)
    corner_right = shifted(jnp.stack((top[:, :tile_len], bottom[:, :tile_len]), 1), "tm", -1)

    cotangent = d_outputs.reshape(query_count, d_outputs.shape[-1])
    d_attended = jnp.zeros((query_count, dim), bf16)
    for step in range(dp_count):
        x = rotated(cotangent, "dp", step) if step else cotangent
        part = contract(x, projection, 1).astype(bf16)
        part = rotated(part, "dp", -step) if step else part
        owner = lax.rem(dp_index + step, dp_count)
        d_attended = lax.dynamic_update_slice_in_dim(d_attended, part, owner * depth, 1)

    bias = window_bias(tile_len, cols, TWIDE)
    pieces = (top, bottom, left, right, corner_left, corner_right)
    attended, d_queries, d_own, *d_pieces = attention(bias, q, k, v, pieces, d_attended)
    d_top, d_bottom, d_left, d_right, d_corner_left, d_corner_right = d_pieces

    corners_high = shifted(d_corner_left, "tm", -1)
    corners_low = shifted(d_corner_right, "tm", 1)
    corners = jnp.concatenate((corners_low, corners_high), axis=2).astype(f32)
    to_top = (d_top.astype(f32) + corners[:, 0]).astype(bf16)
    to_bottom = (d_bottom.astype(f32) + corners[:, 1]).astype(bf16)
    from_bottom = shifted(to_top, "height", -1)
    from_top = shifted(to_bottom, "height", 1)
    from_right = shifted(d_left, "tm", -1)
    from_left = shifted(d_right, "tm", 1)
    summed = d_own + jnp.concatenate((from_left, from_right), axis=1).astype(f32)
    summed = summed + jnp.concatenate((from_top, from_bottom), axis=2).astype(f32)
    summed = summed.astype(bf16)

    outputs = None
    for step in range(dp_count):
        owner = lax.rem(dp_index + step, dp_count)
        x = lax.dynamic_slice_in_dim(attended, owner * depth, depth, 1)
        x = rotated(x, "dp", step) if step else x
        part = contract(x, projection, 0)
        part = rotated(part.astype(bf16), "dp", -step).astype(f32) if step else part
        outputs = part if outputs is None else outputs + part
    outputs = outputs.astype(bf16)
    return (
        outputs.reshape(d_outputs.shape),
        d_queries[None],
        summed[0][None],
        summed[1][None],
    )


def solution(mesh):
    spread = P("dp", "tm", "height", None, None)
    in_specs = (spread, spread, spread, P("dp", None), spread)
    return jax.shard_map(
        body, mesh=mesh, in_specs=in_specs, out_specs=(spread,) * 4, check_vma=False
    )
```

time: 342 us -> 108 us (0.32)
  local copies, waits for them, and re-layouts: 180 us -> 6.11 us
  waiting for transfers between devices: 57.4 us -> 22.9 us
  matrix products: 43.7 us -> 17 us
  Pallas kernels: 0 us -> 17.3 us
  between operations: 14.3 us -> 0.95 us
  starting transfers between devices: 23.5 us -> 35.8 us
  other arithmetic: 13.8 us -> 6.6 us
  loops' own time: 5.66 us -> 0 us
    broadcast_in_dim x8 -> x1, local copies, waits for them, and re-layouts: 69.7 us -> 0.05 us  [body(): d_attended = jnp.zeros((query_count, dim), bf16)]
    dynamic_slice x36 -> x1, local copies, waits for them, and re-layouts: 31.4 us -> 0.02 us  [body(): x = lax.dynamic_slice_in_dim(attended, owner * depth, depth, 1)]
    ppermute x8 -> x16, waiting for transfers between devices: 52.1 us -> 22.9 us  [the longest x12 13.1 us: shifted(): return lax.ppermute(array, axis, pairs)]
    dot_general x22 -> x4, matrix products: 40.9 us -> 17 us  [contract(): lax.dot_general(x, weight, (((1,), (weight_axis,)), ((), ())), preferred_...]
    another operation x7 -> x3, local copies, waits for them, and re-layouts: 22 us -> 1.55 us  [the longest x1 1.46 us: body(): low_rows = jnp.stack((k[:, :tile_len], v[:, :tile_len]))]
    pallas_call x0 -> x1, Pallas kernels: none -> 17.3 us  [attention(): pl.pallas_call(functools.partial(attention_kernel, width // HDIM, 1.0 / m...]
    transpose x3 -> x0, local copies, waits for them, and re-layouts: 16.6 us -> none  [join_groups(): jnp.transpose(stacked, (1, 0, 2))]
    unnamed x19 -> x16, local copies, waits for them, and re-layouts: 16.5 us -> 1.12 us
  transfers between devices with their start and end apart: 9 -> 16, of which waited for: 9 -> 6; matrix products, arithmetic and copies ran while one was open for 37% -> 25% of each run, Pallas kernels for 0% -> 0%
where the time goes in v1:
time: 108 us; the launch traced here: 107 us
  starting transfers between devices  35.8 us (33%)
  waiting for transfers between devices  22.9 us (21%)
  Pallas kernels  17.3 us (16%)
  matrix products  17 us (16%)
  other arithmetic  6.6 us (6%)
  local copies, waits for them, and re-layouts  6.11 us (6%)
    ppermute x12, starting transfers between devices, shifted(): return lax.ppermute(array, axis, pairs)  31.7 us
    pallas_call x1, Pallas kernels, attention(): pl.pallas_call(functools.partial(attention_kernel, width // HDIM, 1.0 / m...  17.3 us
    dot_general x4, matrix products, contract(): lax.dot_general(x, weight, (((1,), (weight_axis,)), ((), ())), preferred_...  17 us
    ppermute x12, waiting for transfers between devices, shifted(): return lax.ppermute(array, axis, pairs)  13.1 us
    ppermute x4, waiting for transfers between devices, rotated(): lax.ppermute(array, axis, [(i, (i + step) % count) for i in range(count)])  9.8 us
    ppermute x4, starting transfers between devices, rotated(): lax.ppermute(array, axis, [(i, (i + step) % count) for i in range(count)])  4.11 us
  transfers between devices with their start and end apart: 16, of which 6 were waited for; matrix products, arithmetic and copies ran while one was open for 25% of the time, Pallas kernels for 0%

profile of v1, /device:TPU:1, one launch (start us, length us, event | category | flops | bytes accessed | tf_op | source)
XLA Modules:
  0.0 106.6 jit_solution(16784055306669974544)
XLA Ops:
  0.6 2.1 %collective-permute-start.6 = (bf16[128,2560]{1,0:T(8,128)(2,1)}, bf16[128,2560]{1,0:T(8,128)(2,1)}, u32[]{:S(2)}, u32[]{:S(2)}) collective-permute-start(bf16[128,2560]{1,0:T(8,128)(2,1)} %bitcast.52), channel_id=1, source_target_pairs={{0,16},{16,0},{1,17},{17,1},{2,18},{18,2},{3,19},{19,3},{4,20},{20... | collective-permute-start | bytes 1966088 | tf_op jit(solution)/shard_map/ppermute | solution.py:183
  2.8 1.5 %slice_bitcast_fusion.6 = (bf16[1,4,2,8,2560]{4,3,2,1,0:T(8,128)(2,1)S(1)}, bf16[1,4,2,8,2560]{4,3,2,1,0:T(8,128)(2,1)S(1)}, bf16[1,4,2,8,2560]{4,3,2,1,0:T(8,128)(2,1)S(1)}, bf16[1,4,2,8,2560]{4,3,2,1,0:T(8,128)(2,1)S(1)}) fusion(bf16[4,4,8,2560]{3,2,1,0:T(8,128)(2,1)} %bitcast.47, bf16[4,4,8,2560]{3,2,1,0:T(8,128)(2,1)} %bitcast.45), kind=kLoop, calls=%fused_computation.24 | loop fusion | bytes 2621440 | tf_op jit(solution)/shard_map/stack | solution.py:201
  5.1 3.2 %collective-permute-start = (bf16[2,4,2,8,2560]{4,3,2,1,0:T(8,128)(2,1)}, bf16[2,4,2,8,2560]{4,3,2,1,0:T(8,128)(2,1)S(1)}, u32[]{:S(2)}, u32[]{:S(2)}) collective-permute-start(bf16[2,4,2,8,2560]{4,3,2,1,0:T(8,128)(2,1)} %pad_maximum_fusion), channel_id=1, source_target_pairs={{0,1},{1,2},{2,3},{4,5},{5,6},{6,7},{8,9},{9,10},{10,11},{12,13},{... | collective-permute-start | bytes 1966088 | tf_op jit(solution)/shard_map/ppermute | solution.py:178
  11.6 4.2 %collective-permute-start.2 = (bf16[2,2,4,8,2560]{4,3,2,1,0:T(8,128)(2,1)}, bf16[2,2,4,8,2560]{4,3,2,1,0:T(8,128)(2,1)}, u32[]{:S(2)}, u32[]{:S(2)}) collective-permute-start(bf16[2,2,4,8,2560]{4,3,2,1,0:T(8,128)(2,1)} %pad_maximum_fusion.2), channel_id=1, source_target_pairs={{0,4},{4,8},{8,12},{1,5},{5,9},{9,13},{2,6},{6,10},{10,14},{3,7},{... | collective-permute-start | bytes 1966088 | tf_op jit(solution)/shard_map/ppermute | solution.py:178
  16.7 1.9 %collective-permute-start.3 = (bf16[2,2,4,8,2560]{4,3,2,1,0:T(8,128)(2,1)}, bf16[2,2,4,8,2560]{4,3,2,1,0:T(8,128)(2,1)}, u32[]{:S(2)}, u32[]{:S(2)}) collective-permute-start(bf16[2,2,4,8,2560]{4,3,2,1,0:T(8,128)(2,1)} %pad_maximum_fusion.3), channel_id=1, source_target_pairs={{4,0},{8,4},{12,8},{5,1},{9,5},{13,9},{6,2},{10,6},{14,10},{7,3},{... | collective-permute-start | bytes 1966088 | tf_op jit(solution)/shard_map/ppermute | solution.py:178
  18.7 5.3 %fusion.1 = bf16[128,2560]{1,0:T(8,128)(2,1)S(1)} fusion(bf16[128,2560]{1,0:T(8,128)(2,1)S(1)} %broadcast_in_dim.18, s32[]{:T(128)S(6)} %select_n.13, bf16[128,2560]{1,0:T(8,128)(2,1)} %bitcast.53, bf16[1280,2560]{1,0:T(8,128)(2,1)} %param.11), kind=kOutput, calls=%fused_computation.6 | convolution fusion | flops 839024640 | bytes 7536644 | tf_op jit(solution)/shard_map/dot_general | solution.py:187
  24.0 6.0 %convolution_convert_fusion.1 = bf16[128,1280]{1,0:T(8,128)(2,1)} fusion(bf16[128,2560]{1,0:T(8,128)(2,1)} %collective-permute-done.6, bf16[1280,2560]{1,0:T(8,128)(2,1)} %param.11), kind=kOutput, calls=%fused_computation.4 | convolution fusion | flops 839024640 | bytes 7536640 | tf_op jit(solution)/shard_map/dot_general | solution.py:187
  31.2 3.9 %collective-permute-start.4 = (bf16[2,2,2,2,8,2560]{5,4,3,2,0,1:T(8,128)(2,1)}, bf16[2,2,2,2,8,2560]{5,4,3,2,0,1:T(8,128)(2,1)}, u32[]{:S(2)}, u32[]{:S(2)}) collective-permute-start(bf16[2,2,2,2,8,2560]{5,4,3,2,0,1:T(8,128)(2,1)} %pad_maximum_fusion.4), channel_id=1, source_target_pairs={{0,4},{4,8},{8,12},{1,5},{5,9},{9,13},{2,6},{6,10},{10,14},{3,7},{... | collective-permute-start | bytes 1966088 | tf_op jit(solution)/shard_map/ppermute | solution.py:178
  36.0 1.9 %collective-permute-start.5 = (bf16[2,2,2,2,8,2560]{5,4,3,2,1,0:T(8,128)(2,1)}, bf16[2,2,2,2,8,2560]{5,4,3,2,1,0:T(8,128)(2,1)}, u32[]{:S(2)}, u32[]{:S(2)}) collective-permute-start(bf16[2,2,2,2,8,2560]{5,4,3,2,1,0:T(8,128)(2,1)} %pad_maximum_fusion.5), channel_id=1, source_target_pairs={{4,0},{8,4},{12,8},{5,1},{9,5},{13,9},{6,2},{10,6},{14,10},{7,3},{... | collective-permute-start | bytes 1966088 | tf_op jit(solution)/shard_map/ppermute | solution.py:178
  39.7 3.3 %collective-permute-done.4 = bf16[2,2,2,2,8,2560]{5,4,3,2,0,1:T(8,128)(2,1)} collective-permute-done((bf16[2,2,2,2,8,2560]{5,4,3,2,0,1:T(8,128)(2,1)}, bf16[2,2,2,2,8,2560]{5,4,3,2,0,1:T(8,128)(2,1)}, u32[]{:S(2)}, u32[]{:S(2)}) %collective-permute-start.4) | collective-permute-done | bytes 655392 | tf_op jit(solution)/shard_map/ppermute | solution.py:178
  44.1 4.1 %collective-permute-done.5.corner_right_ref = bf16[2,2,2,2,8,2560]{5,4,3,2,1,0:T(8,128)(2,1)} collective-permute-done((bf16[2,2,2,2,8,2560]{5,4,3,2,1,0:T(8,128)(2,1)}, bf16[2,2,2,2,8,2560]{5,4,3,2,1,0:T(8,128)(2,1)}, u32[]{:S(2)}, u32[]{:S(2)}) %collective-permute-start.5) | collective-permute-done | bytes 655392 | tf_op jit(solution)/shard_map/ppermute | solution.py:178
  49.3 17.3 %attention.1 = (bf16[128,2560]{1,0:T(8,128)(2,1)S(1)}, bf16[4,4,8,2560]{3,2,1,0:T(8,128)(2,1)}, f32[2,4,4,8,2560]{4,3,2,1,0:T(8,128)S(1)}, bf16[2,4,2,8,2560]{4,...) custom-call(f32[512,128]{1,0:T(8,128)S(1)} %and_select_fusion.bias_r, ...), custom_call_target="tpu_custom_call" | custom-call | flops 2013265920 | bytes 13107200 | tf_op jit(solution)/shard_map/attention/pallas_call | solution.py:159
  66.6 1.3 %collective-permute-start.8 = (bf16[128,1280]{1,0:T(8,128)(2,1)S(1)}, bf16[128,1280]{1,0:T(8,128)(2,1)S(1)}, u32[]{:S(2)}, u32[]{:S(2)}) collective-permute-start(bf16[128,1280]{1,0:T(8,128)(2,1)S(1)} %constant_dynamic-slice_fusion), channel_id=1, source_target_pairs={{0,16},{16,0},{1,17},{17,1},{2,18},{18,2},{3,19},{19,3},{4,20},{20... | collective-permute-start | bytes 983048 | tf_op jit(solution)/shard_map/ppermute | solution.py:183
  67.9 2.0 %collective-permute-start.12 = (bf16[2,2,2,2,8,2560]{5,4,3,2,1,0:T(8,128)(2,1)S(1)}, bf16[2,2,2,2,8,2560]{5,4,3,2,1,0:T(8,128)(2,1)S(1)}, u32[]{:S(2)}, u32[]{:S(2)}) collective-permute-start(bf16[2,2,2,2,8,2560]{5,4,3,2,1,0:T(8,128)(2,1)S(1)} %get-tuple-element.19), channel_id=1, source_target_pairs={{0,4},{4,8},{8,12},{1,5},{5,9},{9,13},{2,6},{6,10},{10,14},{3,7},{... | collective-permute-start | bytes 1966088 | tf_op jit(solution)/shard_map/ppermute | solution.py:178
  69.9 2.3 %collective-permute-start.13 = (bf16[2,2,2,2,8,2560]{5,4,3,2,1,0:T(8,128)(2,1)S(1)}, bf16[2,2,2,2,8,2560]{5,4,3,2,1,0:T(8,128)(2,1)S(1)}, u32[]{:S(2)}, u32[]{:S(2)}) collective-permute-start(bf16[2,2,2,2,8,2560]{5,4,3,2,1,0:T(8,128)(2,1)S(1)} %get-tuple-element.20), channel_id=1, source_target_pairs={{4,0},{8,4},{12,8},{5,1},{9,5},{13,9},{6,2},{10,6},{14,10},{7,3},{... | collective-permute-start | bytes 1966088 | tf_op jit(solution)/shard_map/ppermute | solution.py:178
  72.3 3.2 %collective-permute-start.10 = (bf16[2,2,4,8,2560]{4,3,2,1,0:T(8,128)(2,1)S(1)}, bf16[2,2,4,8,2560]{4,3,2,1,0:T(8,128)(2,1)S(1)}, u32[]{:S(2)}, u32[]{:S(2)}) collective-permute-start(bf16[2,2,4,8,2560]{4,3,2,1,0:T(8,128)(2,1)S(1)} %get-tuple-element.16), channel_id=1, source_target_pairs={{0,4},{4,8},{8,12},{1,5},{5,9},{9,13},{2,6},{6,10},{10,14},{3,7},{... | collective-permute-start | bytes 1966088 | tf_op jit(solution)/shard_map/ppermute | solution.py:178
  75.5 2.1 %collective-permute-start.11 = (bf16[2,2,4,8,2560]{4,3,2,1,0:T(8,128)(2,1)S(1)}, bf16[2,2,4,8,2560]{4,3,2,1,0:T(8,128)(2,1)S(1)}, u32[]{:S(2)}, u32[]{:S(2)}) collective-permute-start(bf16[2,2,4,8,2560]{4,3,2,1,0:T(8,128)(2,1)S(1)} %get-tuple-element.17), channel_id=1, source_target_pairs={{4,0},{8,4},{12,8},{5,1},{9,5},{13,9},{6,2},{10,6},{14,10},{7,3},{... | collective-permute-start | bytes 1966088 | tf_op jit(solution)/shard_map/ppermute | solution.py:178
  77.6 3.9 %convolution_convert_fusion = bf16[128,2560]{1,0:T(8,128)(2,1)S(1)} fusion(bf16[128,1280]{1,0:T(8,128)(2,1)S(1)} %collective-permute-done.8, bf16[1280,2560]{1,0:T(8,128)(2,1)} %param.11), kind=kOutput, calls=%fused_computation.2 | convolution fusion | flops 839188480 | bytes 7536640 | tf_op jit(solution)/shard_map/dot_general | solution.py:187
  82.5 4.3 %collective-permute-start.14 = (bf16[2,4,2,8,2560]{4,3,2,1,0:T(8,128)(2,1)S(1)}, bf16[2,4,2,8,2560]{4,3,2,1,0:T(8,128)(2,1)S(1)}, u32[]{:S(2)}, u32[]{:S(2)}) collective-permute-start(bf16[2,4,2,8,2560]{4,3,2,1,0:T(8,128)(2,1)S(1)} %get-tuple-element.22), channel_id=1, source_target_pairs={{0,1},{1,2},{2,3},{4,5},{5,6},{6,7},{8,9},{9,10},{10,11},{12,13},{... | collective-permute-start | bytes 1966088 | tf_op jit(solution)/shard_map/ppermute | solution.py:178
  86.8 1.3 %collective-permute-start.15 = (bf16[2,4,2,8,2560]{4,3,2,1,0:T(8,128)(2,1)S(1)}, bf16[2,4,2,8,2560]{4,3,2,1,0:T(8,128)(2,1)S(1)}, u32[]{:S(2)}, u32[]{:S(2)}) collective-permute-start(bf16[2,4,2,8,2560]{4,3,2,1,0:T(8,128)(2,1)S(1)} %get-tuple-element.23), channel_id=1, source_target_pairs={{1,0},{2,1},{3,2},{5,4},{6,5},{7,6},{9,8},{10,9},{11,10},{13,12},{... | collective-permute-start | bytes 1966088 | tf_op jit(solution)/shard_map/ppermute | solution.py:178
  88.1 9.2 %collective-permute-done.9 = bf16[128,2560]{1,0:T(8,128)(2,1)S(1)} collective-permute-done((bf16[128,2560]{1,0:T(8,128)(2,1)S(1)}, bf16[128,2560]{1,0:T(8,128)(2,1)S(1)}, u32[]{:S(2)}, u32[]{:S(2)}) %collective-permute-start.9) | collective-permute-done | bytes 655392 | tf_op jit(solution)/shard_map/ppermute | solution.py:183
  97.4 1.9 %fusion = bf16[128,2560]{1,0:T(8,128)(2,1)} fusion(bf16[1280,2560]{1,0:T(8,128)(2,1)S(1)} %bitcast.51, bf16[128,2560]{1,0:T(8,128)(2,1)S(1)} %collective-permute-done.9, bf16[128,2560]{1,0:T(8,128)(2,1)S(1)} %get-tuple-element.13, s32[]{:T(128)S(6)} %select_n.13), kind=kOutput, calls=%fused_computation.1 | convolution fusion | flops 839843840 | bytes 8192004 | tf_op jit(solution)/shard_map/dot_general | solution.py:187
  99.2 1.5 %collective-permute-done.14 = bf16[2,4,2,8,2560]{4,3,2,1,0:T(8,128)(2,1)S(1)} collective-permute-done((bf16[2,4,2,8,2560]{4,3,2,1,0:T(8,128)(2,1)S(1)}, bf16[2,4,2,8,2560]{4,3,2,1,0:T(8,128)(2,1)S(1)}, u32[]{:S(2)}, u32[]{:S(2)}) %collective-permute-start.14) | collective-permute-done | bytes 655392 | tf_op jit(solution)/shard_map/ppermute | solution.py:178
  100.8 4.2 %collective-permute-done.15 = bf16[2,4,2,8,2560]{4,3,2,1,0:T(8,128)(2,1)S(1)} collective-permute-done((bf16[2,4,2,8,2560]{4,3,2,1,0:T(8,128)(2,1)S(1)}, bf16[2,4,2,8,2560]{4,3,2,1,0:T(8,128)(2,1)S(1)}, u32[]{:S(2)}, u32[]{:S(2)}) %collective-permute-start.15) | collective-permute-done | bytes 655392 | tf_op jit(solution)/shard_map/ppermute | solution.py:178
  (50 shorter events, 13.8 us)
Async XLA Ops:
  0.6 23.3 %collective-permute-start.6 = (bf16[128,2560]{1,0:T(8,128)(2,1)}, bf16[128,2560]{1,0:T(8,128)(2,1)}, u32[]{:S(2)}, u32[]{:S(2)}) collective-permute-start(bf16[128,2560]{1,0:T(8,128)(2,1)} %bitcast.52), channel_id=1, source_target_pairs={{0,16},{16,0},{1,17},{17,1},{2,18},{18,2},{3,19},{19,3},{4,20},{20... | collective-permute-start | bytes 1966088 | tf_op jit(solution)/shard_map/ppermute | solution.py:183
  2.8 7.8 %copy-start = (bf16[1,4,4,8,2560]{4,3,2,1,0:T(8,128)(2,1)S(1)}, bf16[1,4,4,8,2560]{4,3,2,1,0:T(8,128)(2,1)}, u32[]{:S(2)}) copy-start(bf16[1,4,4,8,2560]{4,3,2,1,0:T(8,128)(2,1)} %param.9) | copy-start | bytes 1966084
  2.8 7.8 %copy-start.1 = (bf16[1,4,4,8,2560]{4,3,2,1,0:T(8,128)(2,1)S(1)}, bf16[1,4,4,8,2560]{4,3,2,1,0:T(8,128)(2,1)}, u32[]{:S(2)}) copy-start(bf16[1,4,4,8,2560]{4,3,2,1,0:T(8,128)(2,1)} %param.10) | copy-start | bytes 1966084
  5.1 25.1 %collective-permute-start = (bf16[2,4,2,8,2560]{4,3,2,1,0:T(8,128)(2,1)}, bf16[2,4,2,8,2560]{4,3,2,1,0:T(8,128)(2,1)S(1)}, u32[]{:S(2)}, u32[]{:S(2)}) collective-permute-start(bf16[2,4,2,8,2560]{4,3,2,1,0:T(8,128)(2,1)} %pad_maximum_fusion), channel_id=1, source_target_pairs={{0,1},{1,2},{2,3},{4,5},{5,6},{6,7},{8,9},{9,10},{10,11},{12,13},{... | collective-permute-start | bytes 1966088 | tf_op jit(solution)/shard_map/ppermute | solution.py:178
  9.3 21.0 %collective-permute-start.1 = (bf16[2,4,2,8,2560]{4,3,2,1,0:T(8,128)(2,1)}, bf16[2,4,2,8,2560]{4,3,2,1,0:T(8,128)(2,1)S(1)}, u32[]{:S(2)}, u32[]{:S(2)}) collective-permute-start(bf16[2,4,2,8,2560]{4,3,2,1,0:T(8,128)(2,1)} %pad_maximum_fusion.1), channel_id=1, source_target_pairs={{1,0},{2,1},{3,2},{5,4},{6,5},{7,6},{9,8},{10,9},{11,10},{13,12},{... | collective-permute-start | bytes 1966088 | tf_op jit(solution)/shard_map/ppermute | solution.py:178
  11.6 32.5 %collective-permute-start.2 = (bf16[2,2,4,8,2560]{4,3,2,1,0:T(8,128)(2,1)}, bf16[2,2,4,8,2560]{4,3,2,1,0:T(8,128)(2,1)}, u32[]{:S(2)}, u32[]{:S(2)}) collective-permute-start(bf16[2,2,4,8,2560]{4,3,2,1,0:T(8,128)(2,1)} %pad_maximum_fusion.2), channel_id=1, source_target_pairs={{0,4},{4,8},{8,12},{1,5},{5,9},{9,13},{2,6},{6,10},{10,14},{3,7},{... | collective-permute-start | bytes 1966088 | tf_op jit(solution)/shard_map/ppermute | solution.py:178
  16.7 27.4 %collective-permute-start.3 = (bf16[2,2,4,8,2560]{4,3,2,1,0:T(8,128)(2,1)}, bf16[2,2,4,8,2560]{4,3,2,1,0:T(8,128)(2,1)}, u32[]{:S(2)}, u32[]{:S(2)}) collective-permute-start(bf16[2,2,4,8,2560]{4,3,2,1,0:T(8,128)(2,1)} %pad_maximum_fusion.3), channel_id=1, source_target_pairs={{4,0},{8,4},{12,8},{5,1},{9,5},{13,9},{6,2},{10,6},{14,10},{7,3},{... | collective-permute-start | bytes 1966088 | tf_op jit(solution)/shard_map/ppermute | solution.py:178
  30.0 8.0 %copy-start.4 = (s32[512]{0:T(512)S(1)}, s32[512]{0:T(512)}, u32[]{:S(2)}) copy-start(s32[512]{0:T(512)} %constant.47.clone) | copy-start | bytes 6148
  30.0 8.0 %copy-start.5 = (s32[512]{0:T(512)S(1)}, s32[512]{0:T(512)}, u32[]{:S(2)}) copy-start(s32[512]{0:T(512)} %constant.46.clone) | copy-start | bytes 6148
  30.0 8.0 %copy-start.3 = (pred[512,128]{1,0:T(32,128)(4,1)S(1)}, pred[512,128]{1,0:T(32,128)(4,1)}, u32[]{:S(2)}) copy-start(pred[512,128]{1,0:T(32,128)(4,1)} %constant.48.clone) | copy-start | bytes 196612
  30.0 8.7 %collective-permute-start.7 = (bf16[128,1280]{1,0:T(8,128)(2,1)}, bf16[128,1280]{1,0:T(8,128)(2,1)}, u32[]{:S(2)}, u32[]{:S(2)}) collective-permute-start(bf16[128,1280]{1,0:T(8,128)(2,1)} %convolution_convert_fusion.1), channel_id=1, source_target_pairs={{0,16},{16,0},{1,17},{17,1},{2,18},{18,2},{3,19},{19,3},{4,20},{20... | collective-permute-start | bytes 983048 | tf_op jit(solution)/shard_map/ppermute | solution.py:183
  31.2 11.7 %collective-permute-start.4 = (bf16[2,2,2,2,8,2560]{5,4,3,2,0,1:T(8,128)(2,1)}, bf16[2,2,2,2,8,2560]{5,4,3,2,0,1:T(8,128)(2,1)}, u32[]{:S(2)}, u32[]{:S(2)}) collective-permute-start(bf16[2,2,2,2,8,2560]{5,4,3,2,0,1:T(8,128)(2,1)} %pad_maximum_fusion.4), channel_id=1, source_target_pairs={{0,4},{4,8},{8,12},{1,5},{5,9},{9,13},{2,6},{6,10},{10,14},{3,7},{... | collective-permute-start | bytes 1966088 | tf_op jit(solution)/shard_map/ppermute | solution.py:178
  36.0 12.2 %collective-permute-start.5 = (bf16[2,2,2,2,8,2560]{5,4,3,2,1,0:T(8,128)(2,1)}, bf16[2,2,2,2,8,2560]{5,4,3,2,1,0:T(8,128)(2,1)}, u32[]{:S(2)}, u32[]{:S(2)}) collective-permute-start(bf16[2,2,2,2,8,2560]{5,4,3,2,1,0:T(8,128)(2,1)} %pad_maximum_fusion.5), channel_id=1, source_target_pairs={{4,0},{8,4},{12,8},{5,1},{9,5},{13,9},{6,2},{10,6},{14,10},{7,3},{... | collective-permute-start | bytes 1966088 | tf_op jit(solution)/shard_map/ppermute | solution.py:178
  48.2 1.1 %copy-start.2 = (bf16[1,4,4,8,2560]{4,3,2,1,0:T(8,128)(2,1)S(1)}, bf16[1,4,4,8,2560]{4,3,2,1,0:T(8,128)(2,1)}, u32[]{:S(2)}) copy-start(bf16[1,4,4,8,2560]{4,3,2,1,0:T(8,128)(2,1)} %param.8) | copy-start | bytes 1966084
  66.6 30.8 %slice-start = ((s8[6553600]{0:T(1024)(128)(4,1)}), s8[4194304]{0:T(1024)(128)(4,1)S(1)}, s32[]{:S(2)}) async-start(s8[6553600]{0:T(1024)(128)(4,1)} %bitcast.50), calls=%async_computation | async-start | bytes 8388608
  66.6 11.0 %collective-permute-start.8 = (bf16[128,1280]{1,0:T(8,128)(2,1)S(1)}, bf16[128,1280]{1,0:T(8,128)(2,1)S(1)}, u32[]{:S(2)}, u32[]{:S(2)}) collective-permute-start(bf16[128,1280]{1,0:T(8,128)(2,1)S(1)} %constant_dynamic-slice_fusion), channel_id=1, source_target_pairs={{0,16},{16,0},{1,17},{17,1},{2,18},{18,2},{3,19},{19,3},{4,20},{20... | collective-permute-start | bytes 983048 | tf_op jit(solution)/shard_map/ppermute | solution.py:183
  67.9 14.0 %collective-permute-start.12 = (bf16[2,2,2,2,8,2560]{5,4,3,2,1,0:T(8,128)(2,1)S(1)}, bf16[2,2,2,2,8,2560]{5,4,3,2,1,0:T(8,128)(2,1)S(1)}, u32[]{:S(2)}, u32[]{:S(2)}) collective-permute-start(bf16[2,2,2,2,8,2560]{5,4,3,2,1,0:T(8,128)(2,1)S(1)} %get-tuple-element.19), channel_id=1, source_target_pairs={{0,4},{4,8},{8,12},{1,5},{5,9},{9,13},{2,6},{6,10},{10,14},{3,7},{... | collective-permute-start | bytes 1966088 | tf_op jit(solution)/shard_map/ppermute | solution.py:178
  69.9 12.0 %collective-permute-start.13 = (bf16[2,2,2,2,8,2560]{5,4,3,2,1,0:T(8,128)(2,1)S(1)}, bf16[2,2,2,2,8,2560]{5,4,3,2,1,0:T(8,128)(2,1)S(1)}, u32[]{:S(2)}, u32[]{:S(2)}) collective-permute-start(bf16[2,2,2,2,8,2560]{5,4,3,2,1,0:T(8,128)(2,1)S(1)} %get-tuple-element.20), channel_id=1, source_target_pairs={{4,0},{8,4},{12,8},{5,1},{9,5},{13,9},{6,2},{10,6},{14,10},{7,3},{... | collective-permute-start | bytes 1966088 | tf_op jit(solution)/shard_map/ppermute | solution.py:178
  72.3 27.0 %collective-permute-start.10 = (bf16[2,2,4,8,2560]{4,3,2,1,0:T(8,128)(2,1)S(1)}, bf16[2,2,4,8,2560]{4,3,2,1,0:T(8,128)(2,1)S(1)}, u32[]{:S(2)}, u32[]{:S(2)}) collective-permute-start(bf16[2,2,4,8,2560]{4,3,2,1,0:T(8,128)(2,1)S(1)} %get-tuple-element.16), channel_id=1, source_target_pairs={{0,4},{4,8},{8,12},{1,5},{5,9},{9,13},{2,6},{6,10},{10,14},{3,7},{... | collective-permute-start | bytes 1966088 | tf_op jit(solution)/shard_map/ppermute | solution.py:178
  75.5 21.9 %slice-start.1 = ((s8[6553600]{0:T(1024)(128)(4,1)}), s8[2359296]{0:T(1024)(128)(4,1)S(1)}, s32[]{:S(2)}) async-start(s8[6553600]{0:T(1024)(128)(4,1)} %bitcast.50), calls=%async_computation.1 | async-start | bytes 4718592
  75.5 23.7 %collective-permute-start.11 = (bf16[2,2,4,8,2560]{4,3,2,1,0:T(8,128)(2,1)S(1)}, bf16[2,2,4,8,2560]{4,3,2,1,0:T(8,128)(2,1)S(1)}, u32[]{:S(2)}, u32[]{:S(2)}) collective-permute-start(bf16[2,2,4,8,2560]{4,3,2,1,0:T(8,128)(2,1)S(1)} %get-tuple-element.17), channel_id=1, source_target_pairs={{4,0},{8,4},{12,8},{5,1},{9,5},{13,9},{6,2},{10,6},{14,10},{7,3},{... | collective-permute-start | bytes 1966088 | tf_op jit(solution)/shard_map/ppermute | solution.py:178
  81.5 15.9 %collective-permute-start.9 = (bf16[128,2560]{1,0:T(8,128)(2,1)S(1)}, bf16[128,2560]{1,0:T(8,128)(2,1)S(1)}, u32[]{:S(2)}, u32[]{:S(2)}) collective-permute-start(bf16[128,2560]{1,0:T(8,128)(2,1)S(1)} %convolution_convert_fusion), channel_id=1, source_target_pairs={{0,16},{16,0},{1,17},{17,1},{2,18},{18,2},{3,19},{19,3},{4,20},{20... | collective-permute-start | bytes 1966088 | tf_op jit(solution)/shard_map/ppermute | solution.py:183
  82.5 18.2 %collective-permute-start.14 = (bf16[2,4,2,8,2560]{4,3,2,1,0:T(8,128)(2,1)S(1)}, bf16[2,4,2,8,2560]{4,3,2,1,0:T(8,128)(2,1)S(1)}, u32[]{:S(2)}, u32[]{:S(2)}) collective-permute-start(bf16[2,4,2,8,2560]{4,3,2,1,0:T(8,128)(2,1)S(1)} %get-tuple-element.22), channel_id=1, source_target_pairs={{0,1},{1,2},{2,3},{4,5},{5,6},{6,7},{8,9},{9,10},{10,11},{12,13},{... | collective-permute-start | bytes 1966088 | tf_op jit(solution)/shard_map/ppermute | solution.py:178
  86.8 18.1 %collective-permute-start.15 = (bf16[2,4,2,8,2560]{4,3,2,1,0:T(8,128)(2,1)S(1)}, bf16[2,4,2,8,2560]{4,3,2,1,0:T(8,128)(2,1)S(1)}, u32[]{:S(2)}, u32[]{:S(2)}) collective-permute-start(bf16[2,4,2,8,2560]{4,3,2,1,0:T(8,128)(2,1)S(1)} %get-tuple-element.23), channel_id=1, source_target_pairs={{1,0},{2,1},{3,2},{5,4},{6,5},{7,6},{9,8},{10,9},{11,10},{13,12},{... | collective-permute-start | bytes 1966088 | tf_op jit(solution)/shard_map/ppermute | solution.py:178

commit v2 on v1

--- a/solution.py
+++ b/solution.py
@@ -172,21 +172,352 @@
     )(bias, *operands)
 
 
-def shifted(array, axis, step):
-    count = lax.axis_size(axis)
-    pairs = [(i, i + step) for i in range(count) if 0 <= i + step < count]
-    return lax.ppermute(array, axis, pairs)
-
-
-def rotated(array, axis, step):
-    count = lax.axis_size(axis)
-    return lax.ppermute(array, axis, [(i, (i + step) % count) for i in range(count)])
+MESH = pl.DeviceIdType.MESH
+
+
+class Shift:
+    def __init__(self, src, dst, send, recv, axis, step):
+        count, index = lax.axis_size(axis), lax.axis_index(axis)
+        self.has_target = (index + step >= 0) & (index + step < count)
+        self.has_source = (index - step >= 0) & (index - step < count)
+        target = lax.rem(index + step + count, count)
+        self.copy = pltpu.make_async_remote_copy(
+            src_ref=src,
+            dst_ref=dst,
+            send_sem=send,
+            recv_sem=recv,
+            device_id={axis: target},
+            device_id_type=MESH,
+        )
+
+    def start(self):
+        pl.when(self.has_target)(self.copy.start)
+
+    def wait_recv(self):
+        pl.when(self.has_source)(self.copy.wait_recv)
+
+    def wait_send(self):
+        pl.when(self.has_target)(self.copy.wait_send)
+
+
+def rotation(src, dst, send, recv, axis, step):
+    count, index = lax.axis_size(axis), lax.axis_index(axis)
+    target = lax.rem(index + step + count, count)
+    return pltpu.make_async_remote_copy(
+        src_ref=src,
+        dst_ref=dst,
+        send_sem=send,
+        recv_sem=recv,
+        device_id={axis: target},
+        device_id_type=MESH,
+    )
+
+
+def greet():
+    barrier = pltpu.get_barrier_semaphore()
+    expected = 0
+    for axis in ("tm", "height"):
+        count, index = lax.axis_size(axis), lax.axis_index(axis)
+        for step in (-1, 1):
+            there = (index + step >= 0) & (index + step < count)
+            target = lax.rem(index + step + count, count)
+
+            @pl.when(there)
+            def _(axis=axis, target=target):
+                pl.semaphore_signal(
+                    barrier, inc=1, device_id={axis: target}, device_id_type=MESH
+                )
+
+            expected = expected + jnp.where(there, 1, 0)
+    count, index = lax.axis_size("dp"), lax.axis_index("dp")
+    for step in range(1, count):
+        target = lax.rem(index + step, count)
+        pl.semaphore_signal(barrier, inc=1, device_id={"dp": target}, device_id_type=MESH)
+    pl.semaphore_wait(barrier, expected + (count - 1))
+
+
+def tiles_of(width):
+    tile = 2 * HDIM if width % (2 * HDIM) == 0 else width
+    return [slice(i, i + tile) for i in range(0, width, tile)]
 
 
 def contract(x, weight, weight_axis):
     return lax.dot_general(
         x, weight, (((1,), (weight_axis,)), ((), ())), preferred_element_type=jnp.float32
     )
+
+
+def fetch_kernel(
+    k_ref,
+    v_ref,
+    x_ref,
+    w_ref,
+    top_ref,
+    bottom_ref,
+    left_ref,
+    right_ref,
+    corner_left_ref,
+    corner_right_ref,
+    parts_ref,
+    w_held,
+    x_held,
+    x_arrived,
+    part_held,
+    send_sem,
+    recv_sem,
+    local_sem,
+    x_send,
+    x_recv,
+    part_send,
+    part_recv,
+):
+    dp_count = lax.axis_size("dp")
+    half = k_ref.shape[0] // 2
+    greet()
+    first, filled = [], []
+
+    def shift(src, dst, filler, axis, step, into):
+        t = len(first) + (0 if into is first else len(into))
+        move = Shift(src, dst, send_sem.at[t], recv_sem.at[t], axis, step)
+        fill = pltpu.make_async_copy(filler, dst, local_sem.at[t])
+        move.start()
+        pl.when(jnp.logical_not(move.has_source))(fill.start)
+        into.append((move, fill))
+
+    for which, ref in enumerate((k_ref, v_ref)):
+        low, high = ref.at[:, :half], ref.at[:, half:]
+        shift(high, top_ref.at[which], high, "height", 1, first)
+        shift(low, bottom_ref.at[which], low, "height", -1, first)
+    exchange = []
+    for step in range(1, dp_count):
+        s = step - 1
+        move = rotation(x_ref, x_arrived.at[s], x_send.at[s], x_recv.at[s], "dp", step)
+        move.start()
+        exchange.append(move)
+    for which, ref in enumerate((k_ref, v_ref)):
+        low, high = ref.at[:half], ref.at[half:]
+        shift(high, left_ref.at[which], high, "tm", 1, first)
+        shift(low, right_ref.at[which], low, "tm", -1, first)
+    load_w = pltpu.make_async_copy(w_ref, w_held, local_sem.at[12])
+    load_x = pltpu.make_async_copy(x_ref, x_held, local_sem.at[13])
+    load_x.start()
+    load_w.start()
+    load_x.wait()
+    load_w.wait()
+
+    def multiply(block, slot):
+        x = rows_of(block)
+        for tile in tiles_of(w_held.shape[0]):
+            part_held[slot, :, tile] = contract(x, w_held[tile, :], 1).astype(part_held.dtype)
+
+    multiply(x_held[...], 0)
+    keep = pltpu.make_async_copy(part_held.at[0], parts_ref.at[0], local_sem.at[14])
+    keep.start()
+    returned = []
+    for step in range(1, dp_count):
+        s = step - 1
+        exchange[s].wait_recv()
+        multiply(x_arrived[s], step)
+        move = rotation(
+            part_held.at[step], parts_ref.at[step], part_send.at[s], part_recv.at[s], "dp", -step
+        )
+        move.start()
+        returned.append(move)
+
+    def settle(move, fill):
+        move.wait_recv()
+        pl.when(jnp.logical_not(move.has_source))(fill.wait)
+
+    second = []
+    for move, fill in first[:4]:
+        settle(move, fill)
+    for side, ref in enumerate((top_ref, bottom_ref)):
+        low, high = ref.at[:, :half], ref.at[:, half:]
+        shift(high, corner_left_ref.at[:, side], high, "tm", 1, second)
+        shift(low, corner_right_ref.at[:, side], low, "tm", -1, second)
+    for move, fill in first[4:] + second:
+        settle(move, fill)
+    for move, _ in first + second:
+        move.wait_send()
+    for move in exchange:
+        move.wait_send()
+    for move in returned:
+        move.wait()
+    keep.wait()
+
+
+def fetch(k, v, x, w):
+    half = k.shape[0] // 2
+    frames, rows, cols, dim = k.shape
+    others = lax.axis_size("dp") - 1
+    count = frames * rows * cols
+    bf16 = jnp.bfloat16
+    dma = pltpu.SemaphoreType.DMA
+    shapes = [(2, frames, half, cols, dim)] * 2 + [(2, half, rows, cols, dim)] * 2
+    shapes += [(2, 2, half, half, cols, dim)] * 2 + [(others + 1, count, w.shape[0])]
+    anywhere = pl.BlockSpec(memory_space=pl.ANY)
+    slots = max(others, 1)
+    return pl.pallas_call(
+        fetch_kernel,
+        out_shape=[jax.ShapeDtypeStruct(s, bf16) for s in shapes],
+        in_specs=[anywhere] * 4,
+        out_specs=[anywhere] * len(shapes),
+        scratch_shapes=[
+            pltpu.VMEM(w.shape, bf16),
+            pltpu.VMEM(x.shape, bf16),
+            pltpu.VMEM((slots,) + x.shape, bf16),
+            pltpu.VMEM((others + 1, count, w.shape[0]), bf16),
+            dma((12,)),
+            dma((12,)),
+            dma((15,)),
+        ]
+        + [dma((slots,))] * 4,
+        compiler_params=pltpu.CompilerParams(
+            collective_id=0, has_side_effects=True, vmem_limit_bytes=48 * 1024 * 1024
+        ),
+        name="fetch",
+    )(k, v, x, w)
+
+
+def give_kernel(
+    x_ref,
+    w_ref,
+    d_top_ref,
+    d_bottom_ref,
+    d_left_ref,
+    d_right_ref,
+    d_corner_left_ref,
+    d_corner_right_ref,
+    own_ref,
+    arrived_ref,
+    from_top_ref,
+    from_bottom_ref,
+    from_left_ref,
+    from_right_ref,
+    w_held,
+    x_held,
+    x_arrived,
+    y_held,
+    corners_low,
+    corners_high,
+    to_top,
+    to_bottom,
+    send_sem,
+    recv_sem,
+    local_sem,
+    x_send,
+    x_recv,
+    y_send,
+    y_recv,
+):
+    dp_count = lax.axis_size("dp")
+    half = d_left_ref.shape[1]
+    f32 = jnp.float32
+    greet()
+
+    def shift(src, dst, t, axis, step):
+        move = Shift(src, dst, send_sem.at[t], recv_sem.at[t], axis, step)
+        move.start()
+        return move
+
+    corner_moves = [
+        shift(d_corner_left_ref, corners_high, 0, "tm", -1),
+        shift(d_corner_right_ref, corners_low, 1, "tm", 1),
+    ]
+    exchange = []
+    for step in range(1, dp_count):
+        s = step - 1
+        move = rotation(x_ref.at[step], x_arrived.at[s], x_send.at[s], x_recv.at[s], "dp", step)
+        move.start()
+        exchange.append(move)
+    loads = [
+        pltpu.make_async_copy(d_top_ref, to_top, local_sem.at[0]),
+        pltpu.make_async_copy(d_bottom_ref, to_bottom, local_sem.at[1]),
+        pltpu.make_async_copy(x_ref.at[0], x_held, local_sem.at[2]),
+        pltpu.make_async_copy(w_ref, w_held, local_sem.at[3]),
+    ]
+    for load in loads:
+        load.start()
+    for move, ref in zip(corner_moves, (corners_high, corners_low)):
+
+        @pl.when(jnp.logical_not(move.has_source))
+        def _(ref=ref):
+            ref[...] = jnp.zeros_like(ref)
+
+    loads[0].wait()
+    loads[1].wait()
+    for move in corner_moves:
+        move.wait_recv()
+    for side, ref in enumerate((to_top, to_bottom)):
+        for which in range(2):
+            for part, corners in ((slice(0, half), corners_low), (slice(half, 2 * half), corners_high)):
+                total = ref[which, part].astype(f32) + corners[which, side].astype(f32)
+                ref[which, part] = total.astype(ref.dtype)
+    rim_moves = [
+        shift(to_top, from_bottom_ref, 2, "height", -1),
+        shift(to_bottom, from_top_ref, 3, "height", 1),
+        shift(d_left_ref, from_right_ref, 4, "tm", -1),
+        shift(d_right_ref, from_left_ref, 5, "tm", 1),
+    ]
+    loads[2].wait()
+    loads[3].wait()
+    returned = []
+    for step in range(1, dp_count):
+        s = step - 1
+        exchange[s].wait_recv()
+        for tile in tiles_of(w_held.shape[1]):
+            y_held[s, :, tile] = contract(x_arrived[s], w_held[:, tile], 0).astype(y_held.dtype)
+        move = rotation(
+            y_held.at[s], arrived_ref.at[s], y_send.at[s], y_recv.at[s], "dp", -step
+        )
+        move.start()
+        returned.append(move)
+    for tile in tiles_of(w_held.shape[1]):
+        own_ref[:, tile] = contract(x_held[...], w_held[:, tile], 0)
+    for move in rim_moves:
+        move.wait_recv()
+    for move in corner_moves + rim_moves:
+        move.wait_send()
+    for move in exchange:
+        move.wait_send()
+    for move in returned:
+        move.wait()
+
+
+def give(x, w, pieces):
+    top, left, corner = pieces[0].shape, pieces[2].shape, pieces[4].shape
+    others = lax.axis_size("dp") - 1
+    slots = max(others, 1)
+    bf16 = jnp.bfloat16
+    dma = pltpu.SemaphoreType.DMA
+    count, dim = x.shape[1], w.shape[1]
+    outs = [jax.ShapeDtypeStruct((count, dim), jnp.float32)]
+    outs += [jax.ShapeDtypeStruct(s, bf16) for s in ((slots, count, dim), top, top, left, left)]
+    anywhere = pl.BlockSpec(memory_space=pl.ANY)
+    return pl.pallas_call(
+        give_kernel,
+        out_shape=outs,
+        in_specs=[anywhere] * 8,
+        out_specs=[pl.BlockSpec(memory_space=pltpu.VMEM)] + [anywhere] * 5,
+        scratch_shapes=[
+            pltpu.VMEM(w.shape, bf16),
+            pltpu.VMEM(x.shape[1:], bf16),
+            pltpu.VMEM((slots,) + x.shape[1:], bf16),
+            pltpu.VMEM((slots, count, dim), bf16),
+            pltpu.VMEM(corner, bf16),
+            pltpu.VMEM(corner, bf16),
+            pltpu.VMEM(top, bf16),
+            pltpu.VMEM(top, bf16),
+            dma((6,)),
+            dma((6,)),
+            dma((4,)),
+        ]
+        + [dma((slots,))] * 4,
+        compiler_params=pltpu.CompilerParams(
+            collective_id=1, has_side_effects=True, vmem_limit_bytes=48 * 1024 * 1024
+        ),
+        name="give",
+    )(x, w, *pieces)
 
 
 def body(queries, keys, values, projection, d_outputs):
@@ -198,52 +529,38 @@
     depth = projection.shape[0]
     dp_count, dp_index = lax.axis_size("dp"), lax.axis_index("dp")
 
-    low_rows = jnp.stack((k[:, :tile_len], v[:, :tile_len]))
-    high_rows = jnp.stack((k[:, tile_len:], v[:, tile_len:]))
-    low_frames = jnp.stack((k[:tile_len], v[:tile_len]))
-    high_frames = jnp.stack((k[tile_len:], v[tile_len:]))
-    top = shifted(high_rows, "height", 1)
-    bottom = shifted(low_rows, "height", -1)
-    left = shifted(high_frames, "tm", 1)
-    right = shifted(low_frames, "tm", -1)
-    corner_left = shifted(jnp.stack((top[:, tile_len:], bottom[:, tile_len:]), 1), "tm", 1)
-    corner_right = shifted(jnp.stack((top[:, :tile_len], bottom[:, :tile_len]), 1), "tm", -1)
-
-    cotangent = d_outputs.reshape(query_count, d_outputs.shape[-1])
+    *pieces, parts = fetch(k, v, d_outputs[0], projection)
     d_attended = jnp.zeros((query_count, dim), bf16)
     for step in range(dp_count):
-        x = rotated(cotangent, "dp", step) if step else cotangent
-        part = contract(x, projection, 1).astype(bf16)
-        part = rotated(part, "dp", -step) if step else part
         owner = lax.rem(dp_index + step, dp_count)
-        d_attended = lax.dynamic_update_slice_in_dim(d_attended, part, owner * depth, 1)
+        d_attended = lax.dynamic_update_slice_in_dim(d_attended, parts[step], owner * depth, 1)
 
     bias = window_bias(tile_len, cols, TWIDE)
-    pieces = (top, bottom, left, right, corner_left, corner_right)
     attended, d_queries, d_own, *d_pieces = attention(bias, q, k, v, pieces, d_attended)
-    d_top, d_bottom, d_left, d_right, d_corner_left, d_corner_right = d_pieces
-
-    corners_high = shifted(d_corner_left, "tm", -1)
-    corners_low = shifted(d_corner_right, "tm", 1)
-    corners = jnp.concatenate((corners_low, corners_high), axis=2).astype(f32)
-    to_top = (d_top.astype(f32) + corners[:, 0]).astype(bf16)
-    to_bottom = (d_bottom.astype(f32) + corners[:, 1]).astype(bf16)
-    from_bottom = shifted(to_top, "height", -1)
-    from_top = shifted(to_bottom, "height", 1)
-    from_right = shifted(d_left, "tm", -1)
-    from_left = shifted(d_right, "tm", 1)
-    summed = d_own + jnp.concatenate((from_left, from_right), axis=1).astype(f32)
-    summed = summed + jnp.concatenate((from_top, from_bottom), axis=2).astype(f32)
-    summed = summed.astype(bf16)
-
-    outputs = None
+
+    sliced = []
     for step in range(dp_count):
         owner = lax.rem(dp_index + step, dp_count)
-        x = lax.dynamic_slice_in_dim(attended, owner * depth, depth, 1)
-        x = rotated(x, "dp", step) if step else x
-        part = contract(x, projection, 0)
-        part = rotated(part.astype(bf16), "dp", -step).astype(f32) if step else part
-        outputs = part if outputs is None else outputs + part
+        sliced.append(lax.dynamic_slice_in_dim(attended, owner * depth, depth, 1))
+    own, arrived, from_top, from_bottom, from_left, from_right = give(
+        jnp.stack(sliced), projection, d_pieces
+    )
+
+    def present(array, axis, step):
+        index = lax.axis_index(axis)
+        there = (index - step >= 0) & (index - step < lax.axis_size(axis))
+        return jnp.where(there, array.astype(f32), 0.0)
+
+    summed = d_own + jnp.concatenate(
+        (present(from_left, "tm", 1), present(from_right, "tm", -1)), axis=1
+    )
+    summed = summed + jnp.concatenate(
+        (present(from_top, "height", 1), present(from_bottom, "height", -1)), axis=2
+    )
+    summed = summed.astype(bf16)
+    outputs = own
+    for step in range(1, dp_count):
+        outputs = outputs + arrived[step - 1].astype(f32)
     outputs = outputs.astype(bf16)
     return (
         outputs.reshape(d_outputs.shape),

time: 108 us -> 110 us (1.019)
  Pallas kernels: 17.3 us -> 76.3 us
  starting transfers between devices: 35.8 us -> 0 us
  waiting for transfers between devices: 22.9 us -> 0 us
  local copies, waits for them, and re-layouts: 6.11 us -> 24.9 us
  matrix products: 17 us -> 0 us
    pallas_call x0 -> x2, Pallas kernels: none -> 59.5 us  [the longest x1 31.7 us: fetch(): pl.pallas_call(fetch_kernel, out_shape=[jax.ShapeDtypeStruct(s, bf16) for...]
    ppermute x16 -> x0, starting transfers between devices: 35.8 us -> none  [the longest x12 31.7 us: shifted(): return lax.ppermute(array, axis, pairs)]
    ppermute x16 -> x0, waiting for transfers between devices: 22.9 us -> none  [the longest x12 13.1 us: shifted(): return lax.ppermute(array, axis, pairs)]
    unnamed x16 -> x64, local copies, waits for them, and re-layouts: 1.12 us -> 23.6 us
    dot_general x4 -> x0, matrix products: 17 us -> none  [contract(): lax.dot_general(x, weight, (((1,), (weight_axis,)), ((), ())), preferred_...]
    another operation x6 -> x1, other arithmetic: 5.37 us -> 0.06 us  [body(): jnp.stack(sliced)]
    select_n x0 -> x2, other arithmetic: none -> 4.82 us  [present(): return jnp.where(there, array.astype(f32), 0.0)]
    another operation x3 -> x1, local copies, waits for them, and re-layouts: 1.55 us -> 0.04 us  [body(): jnp.stack(sliced)]
  transfers between devices with their start and end apart: 16 -> 0, of which waited for: 6 -> 0; matrix products, arithmetic and copies ran while one was open for 25% -> 0% of each run, Pallas kernels for 0% -> 0%
where the time goes in v2:
time: 110 us; the launch traced here: 109 us
  Pallas kernels  76.3 us (69%)
  local copies, waits for them, and re-layouts  24.9 us (23%)
  other arithmetic  6.83 us (6%)
    pallas_call x1, Pallas kernels, fetch(): pl.pallas_call(fetch_kernel, out_shape=[jax.ShapeDtypeStruct(s, bf16) for...  31.7 us
    pallas_call x1, Pallas kernels, give(): pl.pallas_call(give_kernel, out_shape=outs, in_specs=[anywhere] * 8, out_...  27.8 us
    unnamed x64, local copies, waits for them, and re-layouts  23.6 us
    pallas_call x1, Pallas kernels, attention(): pl.pallas_call(functools.partial(attention_kernel, width // HDIM, 1.0 / m...  16.7 us
    select_n x2, other arithmetic, present(): return jnp.where(there, array.astype(f32), 0.0)  4.82 us

profile of v2, /device:TPU:1, one launch (start us, length us, event | category | flops | bytes accessed | tf_op | source)
XLA Modules:
  0.0 108.8 jit_solution(17537190502944536157)
XLA Ops:
  0.7 1.1 copy-done
  1.7 1.1 copy-done.2
  2.8 31.7 %fetch.1 = (bf16[2,4,2,8,2560]{4,3,2,1,0:T(8,128)(2,1)S(1)}, bf16[2,4,2,8,2560]{4,3,2,1,0:T(8,128)(2,1)S(1)}, bf16[2,2,4,8,2560]{4,3,2,1,0:T(8,128)(2,1)S(1)}, b...) custom-call(bf16[4,4,8,2560]{3,2,1,0:T(8,128)(2,1)S(1)} %bitcast.17,, ...), custom_call_target="tpu_custom_call" | custom-call | tf_op jit(solution)/shard_map/fetch/pallas_call | solution.py:360
  35.4 0.8 copy-done.16
  36.2 0.8 copy-done.18
  37.9 0.9 copy-done.22
  38.7 0.9 copy-done.24
  41.0 1.1 copy-done.3
  42.1 1.1 copy-done.5
  43.2 1.1 copy-done.13
  44.2 1.1 copy-done.15
  45.3 1.1 copy-done.17
  46.4 1.1 copy-done.19
  47.5 1.1 copy-done.21
  48.6 1.1 copy-done.23
  49.7 1.1 copy-done.25
  50.8 16.7 %attention.1 = (bf16[128,2560]{1,0:T(8,128)(2,1)S(1)}, bf16[4,4,8,2560]{3,2,1,0:T(8,128)(2,1)}, f32[2,4,4,8,2560]{4,3,2,1,0:T(8,128)S(1)}, bf16[2,4,2,8,2560]{4,...) custom-call(f32[512,128]{1,0:T(8,128)S(1)} %and_select_fusion.bias_r, ...), custom_call_target="tpu_custom_call" | custom-call | flops 2013265920 | bytes 13107200 | tf_op jit(solution)/shard_map/attention/pallas_call | solution.py:159
  68.8 27.8 %give.1 = (f32[128,2560]{1,0:T(8,128)}, bf16[1,128,2560]{2,1,0:T(8,128)(2,1)S(1)}, bf16[2,4,2,8,2560]{4,3,2,1,0:T(8,128)(2,1)S(1)}, bf16[2,4,2,8,2560]{4,3,2,1,0...) custom-call(bf16[2,128,1280]{2,1,0:T(8,128)(2,1)S(1)} %pad_maximum_fusion.x_ref, ...), custom_call_target="tpu_custom_call" | custom-call | tf_op jit(solution)/shard_map/give/pallas_call | solution.py:497
  98.3 0.9 copy-done.8
  100.0 3.1 %convert_select_fusion = (f32[2,4,2,8,2560]{4,3,2,1,0:T(8,128)}, f32[2,4,2,8,2560]{4,3,2,1,0:T(8,128)}) fusion(bf16[2,4,2,8,2560]{4,3,2,1,0:T(8,128)(2,1)} %copy-done.9, pred[]{:T(512)S(6)} %and.45, bf16[2,4,2,8,2560]{4,3,2,1,0:T(8,128)(2,1)} %copy-done.8, pred[]{:T(512)S(6)} %and.44), kind=kLoop, calls=%fused_computation.5 | loop fusion | flops 1310720 | bytes 3932162 | tf_op jit(solution)/shard_map/jit(_where)/select_n | solution.py:552
  103.1 1.7 %convert_select_fusion.2 = (f32[2,2,4,8,2560]{4,3,2,1,0:T(8,128)S(1)}, f32[2,2,4,8,2560]{4,3,2,1,0:T(8,128)S(1)}) fusion(bf16[2,2,4,8,2560]{4,3,2,1,0:T(8,128)(2,1)} %copy-done.7, pred[]{:T(512)S(6)} %and.43, bf16[2,2,4,8,2560]{4,3,2,1,0:T(8,128)(2,1)} %copy-done.6, pred[]{:T(512)S(6)} %and.42), kind=kLoop, calls=%fused_computation.7 | loop fusion | flops 1310720 | bytes 3932162 | tf_op jit(solution)/shard_map/jit(_where)/select_n | solution.py:552
  105.2 0.8 fusion.1
  106.0 1.1 %fusion.10 = (bf16[1,4,4,8,2560]{4,3,2,1,0:T(8,128)(2,1)}, bf16[1,4,4,8,2560]{4,3,2,1,0:T(8,128)(2,1)}) fusion(bf16[2,4,4,8,2560]{4,3,2,1,0:T(8,128)(2,1)S(1)} %fusion.1), kind=kLoop, calls=%fused_computation.24 | loop fusion | bytes 2621440 | tf_op jit(solution)/shard_map/slice | solution.py:569
  107.8 1.0 fusion.2
  (55 shorter events, 7.8 us)
Async XLA Ops:
  0.6 1.1 %copy-start = (bf16[1,4,4,8,2560]{4,3,2,1,0:T(8,128)(2,1)S(1)}, bf16[1,4,4,8,2560]{4,3,2,1,0:T(8,128)(2,1)}, u32[]{:S(2)}) copy-start(bf16[1,4,4,8,2560]{4,3,2,1,0:T(8,128)(2,1)} %param.9) | copy-start | bytes 1966084
  1.7 1.1 copy-start.2
  34.5 0.8 copy-start.14
  37.9 0.9 copy-start.22
  38.7 0.9 copy-start.24
  39.6 1.0 copy-start.30
  39.6 1.0 copy-start.31
  39.6 1.0 copy-start.29
  39.6 1.4 %copy-start.1 = (bf16[1,4,4,8,2560]{4,3,2,1,0:T(8,128)(2,1)S(1)}, bf16[1,4,4,8,2560]{4,3,2,1,0:T(8,128)(2,1)}, u32[]{:S(2)}) copy-start(bf16[1,4,4,8,2560]{4,3,2,1,0:T(8,128)(2,1)} %param.9) | copy-start | bytes 1966084
  41.0 1.1 copy-start.3
  42.1 1.1 copy-start.5
  43.1 1.1 copy-start.13
  44.2 1.1 copy-start.15
  45.3 1.1 copy-start.17
  46.4 1.1 copy-start.19
  47.5 1.1 copy-start.21
  48.6 1.1 copy-start.23
  49.7 1.1 copy-start.25
  67.5 1.0 copy-start.11
  67.5 1.3 %copy-start.12 = (bf16[2,2,2,2,8,2560]{5,4,3,2,1,0:T(8,128)(2,1)}, bf16[2,2,2,2,8,2560]{5,4,3,2,1,0:T(8,128)(2,1)S(1)}, u32[]{:S(2)}) copy-start(bf16[2,2,2,2,8,2560]{5,4,3,2,1,0:T(8,128)(2,1)S(1)} %get-tuple-element.39.d_corner_right_ref) | copy-start | bytes 1966084
  98.3 0.9 copy-start.8
  103.1 1.8 %copy-start.26 = (f32[2,4,2,8,2560]{4,3,2,1,0:T(8,128)S(1)}, f32[2,4,2,8,2560]{4,3,2,1,0:T(8,128)}, u32[]{:S(2)}) copy-start(f32[2,4,2,8,2560]{4,3,2,1,0:T(8,128)} %get-tuple-element.52) | copy-start | bytes 3932164
  103.1 2.1 %copy-start.27 = (f32[2,4,2,8,2560]{4,3,2,1,0:T(8,128)S(1)}, f32[2,4,2,8,2560]{4,3,2,1,0:T(8,128)}, u32[]{:S(2)}) copy-start(f32[2,4,2,8,2560]{4,3,2,1,0:T(8,128)} %get-tuple-element.53) | copy-start | bytes 3932164
  106.0 1.8 %copy-start.28 = (f32[128,2560]{1,0:T(8,128)S(1)}, f32[128,2560]{1,0:T(8,128)}, u32[]{:S(2)}) copy-start(f32[128,2560]{1,0:T(8,128)} %get-tuple-element.40) | copy-start | bytes 3932164
  (8 other events, 6.7 us)

commit v3 on v2

--- a/solution.py
+++ b/solution.py
@@ -15,6 +15,7 @@
 TILES_W = 2
 
 FAR = -1e30
+VMEM_LIMIT = 60 * 1024 * 1024
 
 
 def key_tiles():
@@ -162,7 +163,7 @@
         out_shape=outs,
         in_specs=[pl.BlockSpec(bias.shape, lambda i: (0, 0))] + [blocked(a) for a in operands],
         out_specs=[blocked(o) for o in outs],
-        compiler_params=pltpu.CompilerParams(vmem_limit_bytes=40 * 1024 * 1024),
+        compiler_params=pltpu.CompilerParams(vmem_limit_bytes=VMEM_LIMIT),
         cost_estimate=pl.CostEstimate(
             flops=12 * keys * queries * dim,
             bytes_accessed=moved,
@@ -355,7 +356,7 @@
     dma = pltpu.SemaphoreType.DMA
     shapes = [(2, frames, half, cols, dim)] * 2 + [(2, half, rows, cols, dim)] * 2
     shapes += [(2, 2, half, half, cols, dim)] * 2 + [(others + 1, count, w.shape[0])]
-    anywhere = pl.BlockSpec(memory_space=pl.ANY)
+    anywhere = pl.BlockSpec(memory_space=pltpu.HBM)
     slots = max(others, 1)
     return pl.pallas_call(
         fetch_kernel,
@@ -373,7 +374,7 @@
         ]
         + [dma((slots,))] * 4,
         compiler_params=pltpu.CompilerParams(
-            collective_id=0, has_side_effects=True, vmem_limit_bytes=48 * 1024 * 1024
+            collective_id=0, has_side_effects=True, vmem_limit_bytes=VMEM_LIMIT
         ),
         name="fetch",
     )(k, v, x, w)
@@ -493,7 +494,7 @@
     count, dim = x.shape[1], w.shape[1]
     outs = [jax.ShapeDtypeStruct((count, dim), jnp.float32)]
     outs += [jax.ShapeDtypeStruct(s, bf16) for s in ((slots, count, dim), top, top, left, left)]
-    anywhere = pl.BlockSpec(memory_space=pl.ANY)
+    anywhere = pl.BlockSpec(memory_space=pltpu.HBM)
     return pl.pallas_call(
         give_kernel,
         out_shape=outs,
@@ -514,7 +515,7 @@
         ]
         + [dma((slots,))] * 4,
         compiler_params=pltpu.CompilerParams(
-            collective_id=1, has_side_effects=True, vmem_limit_bytes=48 * 1024 * 1024
+            collective_id=1, has_side_effects=True, vmem_limit_bytes=VMEM_LIMIT
         ),
         name="give",
     )(x, w, *pieces)

time: 110 us -> 122 us (1.11)
  Pallas kernels: 76.3 us -> 109 us
  local copies, waits for them, and re-layouts: 24.9 us -> 4.62 us
    pallas_call x1, Pallas kernels: 27.8 us -> 57.9 us  [give(): pl.pallas_call(give_kernel, out_shape=outs, in_specs=[anywhere] * 8, out_...]
    unnamed x64 -> x18, local copies, waits for them, and re-layouts: 23.6 us -> 1.23 us
    pallas_call x1, Pallas kernels: 31.7 us -> 34.2 us  [fetch(): pl.pallas_call(fetch_kernel, out_shape=[jax.ShapeDtypeStruct(s, bf16) for...]
    select_n x2, other arithmetic: 4.82 us -> 3.2 us  [present(): return jnp.where(there, array.astype(f32), 0.0)]
where the time goes in v3:
time: 122 us; the launch traced here: 121 us
  Pallas kernels  109 us (89%)
  other arithmetic  6.73 us (6%)
  local copies, waits for them, and re-layouts  4.62 us (4%)
    pallas_call x1, Pallas kernels, give(): pl.pallas_call(give_kernel, out_shape=outs, in_specs=[anywhere] * 8, out_...  57.9 us
    pallas_call x1, Pallas kernels, fetch(): pl.pallas_call(fetch_kernel, out_shape=[jax.ShapeDtypeStruct(s, bf16) for...  34.2 us
    pallas_call x1, Pallas kernels, attention(): pl.pallas_call(functools.partial(attention_kernel, width // HDIM, 1.0 / m...  17 us
    select_n x2, other arithmetic, present(): return jnp.where(there, array.astype(f32), 0.0)  3.2 us

profile of v3, /device:TPU:1, one launch (start us, length us, event | category | flops | bytes accessed | tf_op | source)
XLA Modules:
  0.0 121.3 jit_solution(7063779986365243423)
XLA Ops:
  0.6 34.2 %fetch.1 = (bf16[2,4,2,8,2560]{4,3,2,1,0:T(8,128)(2,1)}, bf16[2,4,2,8,2560]{4,3,2,1,0:T(8,128)(2,1)}, bf16[2,2,4,8,2560]{4,3,2,1,0:T(8,128)(2,1)}, bf16[2,2,4,8,...) custom-call(bf16[4,4,8,2560]{3,2,1,0:T(8,128)(2,1)} %bitcast.18, ...), custom_call_target="tpu_custom_call" | custom-call | tf_op jit(solution)/shard_map/fetch/pallas_call | solution.py:361
  34.8 0.0 copy-start.4
  34.9 0.0 copy-start.7
  34.9 0.0 copy-start.8
  34.9 0.0 copy-start.6
  34.9 1.1 bitcast_dynamic-update-slice_fusion.1
  36.0 0.0 copy-done.4
  36.1 0.0 copy-start.3
  36.1 0.0 copy-done.6
  36.1 0.8 and_select_fusion.bias_ref
  37.0 17.0 %attention.1 = (bf16[128,2560]{1,0:T(8,128)(2,1)}, bf16[4,4,8,2560]{3,2,1,0:T(8,128)(2,1)}, f32[2,4,4,8,2560]{4,3,2,1,0:T(8,128)}, bf16[2,4,2,8,2560]{4,3,2,1,0:...) custom-call(f32[512,128]{1,0:T(8,128)} %and_select_fusion.bias_ref, ...), custom_call_target="tpu_custom_call" | custom-call | flops 2013265920 | bytes 13107200 | tf_op jit(solution)/shard_map/attention/pallas_call | solution.py:160
  54.0 1.1 dynamic-slice_bitcast_fusion.1
  55.1 0.9 pad_maximum_fusion.x_ref
  56.0 57.9 %give.1 = (f32[128,2560]{1,0:T(8,128)}, bf16[1,128,2560]{2,1,0:T(8,128)(2,1)}, bf16[2,4,2,8,2560]{4,3,2,1,0:T(8,128)(2,1)}, bf16[2,4,2,8,2560]{4,3,2,1,0:T(8,128...) custom-call(bf16[2,128,1280]{2,1,0:T(8,128)(2,1)} %pad_maximum_fusion.x_ref, ...), custom_call_target="tpu_custom_call" | custom-call | tf_op jit(solution)/shard_map/give/pallas_call | solution.py:498
  113.9 1.7 %convert_select_fusion = (f32[2,4,2,8,2560]{4,3,2,1,0:T(8,128)S(1)}, f32[2,4,2,8,2560]{4,3,2,1,0:T(8,128)S(1)}) fusion(bf16[2,4,2,8,2560]{4,3,2,1,0:T(8,128)(2,1)} %get-tuple-element.47, pred[]{:T(512)S(6)} %and.45, bf16[2,4,2,8,2560]{4,3,2,1,0:T(8,128)(2,1)} %get-tuple-element.46, pred[]{:T(512)S(6)} %and.44), kind=kLoop, calls=%fused_computation.5 | loop fusion | flops 1310720 | bytes 3932162 | tf_op jit(solution)/shard_map/jit(_where)/select_n | solution.py:553
  115.6 0.0 copy-done.5
  115.6 0.0 copy-start
  115.6 1.5 %convert_select_fusion.2 = (f32[2,2,4,8,2560]{4,3,2,1,0:T(8,128)S(1)}, f32[2,2,4,8,2560]{4,3,2,1,0:T(8,128)S(1)}) fusion(bf16[2,2,4,8,2560]{4,3,2,1,0:T(8,128)(2,1)} %get-tuple-element.45, pred[]{:T(512)S(6)} %and.43, bf16[2,2,4,8,2560]{4,3,2,1,0:T(8,128)(2,1)S(1)} %copy-done.5, pred[]{:T(512)S(6)} %and.42), kind=kLoop, calls=%fused_computation.7 | loop fusion | flops 1310720 | bytes 3932162 | tf_op jit(solution)/shard_map/jit(_where)/select_n | solution.py:553
  117.2 0.4 copy-done
  117.5 0.8 fusion.1
  118.4 1.1 fusion.10
  119.5 0.6 copy-done.1
  120.2 0.2 copy-done.2
  120.3 0.9 fusion.2
  (9 shorter events, 0.1 us)
Async XLA Ops:
  34.8 1.2 copy-start.4
  34.9 1.2 %copy-start.7 = (s32[512]{0:T(512)S(1)}, s32[512]{0:T(512)}, u32[]{:S(2)}) copy-start(s32[512]{0:T(512)} %constant.53.clone) | copy-start | bytes 6148
  34.9 1.2 %copy-start.8 = (s32[512]{0:T(512)S(1)}, s32[512]{0:T(512)}, u32[]{:S(2)}) copy-start(s32[512]{0:T(512)} %constant.54.clone) | copy-start | bytes 6148
  34.9 1.2 %copy-start.6 = (pred[512,128]{1,0:T(32,128)(4,1)S(1)}, pred[512,128]{1,0:T(32,128)(4,1)}, u32[]{:S(2)}) copy-start(pred[512,128]{1,0:T(32,128)(4,1)} %constant.55.clone) | copy-start | bytes 196612
  36.1 0.9 copy-start.3
  113.9 1.7 %copy-start.5 = (bf16[2,2,4,8,2560]{4,3,2,1,0:T(8,128)(2,1)S(1)}, bf16[2,2,4,8,2560]{4,3,2,1,0:T(8,128)(2,1)}, u32[]{:S(2)}) copy-start(bf16[2,2,4,8,2560]{4,3,2,1,0:T(8,128)(2,1)} %get-tuple-element.44) | copy-start | bytes 1966084
  115.6 1.9 %copy-start = (f32[2,4,4,8,2560]{4,3,2,1,0:T(8,128)S(1)}, f32[2,4,4,8,2560]{4,3,2,1,0:T(8,128)}, u32[]{:S(2)}) copy-start(f32[2,4,4,8,2560]{4,3,2,1,0:T(8,128)} %get-tuple-element.43) | copy-start | bytes 7864324
  118.4 1.8 %copy-start.1 = (f32[128,2560]{1,0:T(8,128)S(1)}, f32[128,2560]{1,0:T(8,128)}, u32[]{:S(2)}) copy-start(f32[128,2560]{1,0:T(8,128)} %get-tuple-element.40) | copy-start | bytes 3932164
  118.4 1.9 %copy-start.2 = (bf16[1,128,2560]{2,1,0:T(8,128)(2,1)S(1)}, bf16[1,128,2560]{2,1,0:T(8,128)(2,1)}, u32[]{:S(2)}) copy-start(bf16[1,128,2560]{2,1,0:T(8,128)(2,1)} %get-tuple-element.41) | copy-start | bytes 1966084

commit v4 on v3

--- a/solution.py
+++ b/solution.py
@@ -381,22 +381,26 @@
 
 
 def give_kernel(
+    w_ref,
+    d_own_ref,
     x_ref,
-    w_ref,
-    d_top_ref,
-    d_bottom_ref,
+    to_top_ref,
+    to_bottom_ref,
     d_left_ref,
     d_right_ref,
     d_corner_left_ref,
     d_corner_right_ref,
+    outputs_ref,
+    dk_ref,
+    dv_ref,
     own_ref,
+    total_ref,
     arrived_ref,
     from_top_ref,
     from_bottom_ref,
     from_left_ref,
     from_right_ref,
     w_held,
-    x_held,
     x_arrived,
     y_held,
     corners_low,
@@ -432,10 +436,8 @@
         move.start()
         exchange.append(move)
     loads = [
-        pltpu.make_async_copy(d_top_ref, to_top, local_sem.at[0]),
-        pltpu.make_async_copy(d_bottom_ref, to_bottom, local_sem.at[1]),
-        pltpu.make_async_copy(x_ref.at[0], x_held, local_sem.at[2]),
-        pltpu.make_async_copy(w_ref, w_held, local_sem.at[3]),
+        pltpu.make_async_copy(w_ref, w_held, local_sem.at[0]),
+        pltpu.make_async_copy(d_own_ref, total_ref, local_sem.at[1]),
     ]
     for load in loads:
         load.start()
@@ -445,23 +447,27 @@
         def _(ref=ref):
             ref[...] = jnp.zeros_like(ref)
 
-    loads[0].wait()
-    loads[1].wait()
     for move in corner_moves:
         move.wait_recv()
-    for side, ref in enumerate((to_top, to_bottom)):
+    for side, (ref, sent) in enumerate(((to_top_ref, to_top), (to_bottom_ref, to_bottom))):
         for which in range(2):
             for part, corners in ((slice(0, half), corners_low), (slice(half, 2 * half), corners_high)):
                 total = ref[which, part].astype(f32) + corners[which, side].astype(f32)
-                ref[which, part] = total.astype(ref.dtype)
+                sent[which, part] = total.astype(sent.dtype)
     rim_moves = [
         shift(to_top, from_bottom_ref, 2, "height", -1),
         shift(to_bottom, from_top_ref, 3, "height", 1),
         shift(d_left_ref, from_right_ref, 4, "tm", -1),
         shift(d_right_ref, from_left_ref, 5, "tm", 1),
     ]
-    loads[2].wait()
-    loads[3].wait()
+    rim_refs = (from_bottom_ref, from_top_ref, from_right_ref, from_left_ref)
+    for move, ref in zip(rim_moves, rim_refs):
+
+        @pl.when(jnp.logical_not(move.has_source))
+        def _(ref=ref):
+            ref[...] = jnp.zeros_like(ref)
+
+    loads[0].wait()
     returned = []
     for step in range(1, dp_count):
         s = step - 1
@@ -474,35 +480,55 @@
         move.start()
         returned.append(move)
     for tile in tiles_of(w_held.shape[1]):
-        own_ref[:, tile] = contract(x_held[...], w_held[:, tile], 0)
+        own_ref[:, tile] = contract(x_ref[0], w_held[:, tile], 0)
+    loads[1].wait()
     for move in rim_moves:
         move.wait_recv()
-    for move in corner_moves + rim_moves:
+    halves = (slice(0, half), slice(half, 2 * half))
+    for which, ref in enumerate((dk_ref, dv_ref)):
+        for f, from_frames in zip(halves, (from_left_ref, from_right_ref)):
+            for r, from_rows in zip(halves, (from_top_ref, from_bottom_ref)):
+                total = total_ref[which, f, r] + from_frames[which, :, r].astype(f32)
+                total = total + from_rows[which, f].astype(f32)
+                ref[f, r] = total.astype(ref.dtype)
+    for move in returned:
+        move.wait_recv()
+    for tile in tiles_of(w_held.shape[1]):
+        total = own_ref[:, tile]
+        for s in range(dp_count - 1):
+            total = total + arrived_ref[s, :, tile].astype(f32)
+        shape = outputs_ref.shape[:-1] + total.shape[-1:]
+        outputs_ref[:, :, :, tile] = total.reshape(shape).astype(outputs_ref.dtype)
+    for move in corner_moves + rim_moves + exchange + returned:
         move.wait_send()
-    for move in exchange:
-        move.wait_send()
-    for move in returned:
-        move.wait()
-
-
-def give(x, w, pieces):
+
+
+def give(x, w, d_own, pieces):
     top, left, corner = pieces[0].shape, pieces[2].shape, pieces[4].shape
     others = lax.axis_size("dp") - 1
     slots = max(others, 1)
     bf16 = jnp.bfloat16
     dma = pltpu.SemaphoreType.DMA
     count, dim = x.shape[1], w.shape[1]
-    outs = [jax.ShapeDtypeStruct((count, dim), jnp.float32)]
-    outs += [jax.ShapeDtypeStruct(s, bf16) for s in ((slots, count, dim), top, top, left, left)]
+    grid = d_own.shape[1:-1]
+    outs = [jax.ShapeDtypeStruct(grid + (dim,), bf16)]
+    outs += [jax.ShapeDtypeStruct(d_own.shape[1:], bf16)] * 2
     anywhere = pl.BlockSpec(memory_space=pltpu.HBM)
+    inside = pl.BlockSpec(memory_space=pltpu.VMEM)
     return pl.pallas_call(
         give_kernel,
         out_shape=outs,
-        in_specs=[anywhere] * 8,
-        out_specs=[pl.BlockSpec(memory_space=pltpu.VMEM)] + [anywhere] * 5,
+        in_specs=[anywhere] * 2 + [inside] * 7,
+        out_specs=[inside] * 3,
         scratch_shapes=[
+            pltpu.VMEM((count, dim), jnp.float32),
+            pltpu.VMEM(d_own.shape, jnp.float32),
+            pltpu.VMEM((slots, count, dim), bf16),
+            pltpu.VMEM(top, bf16),
+            pltpu.VMEM(top, bf16),
+            pltpu.VMEM(left, bf16),
+            pltpu.VMEM(left, bf16),
             pltpu.VMEM(w.shape, bf16),
-            pltpu.VMEM(x.shape[1:], bf16),
             pltpu.VMEM((slots,) + x.shape[1:], bf16),
             pltpu.VMEM((slots, count, dim), bf16),
             pltpu.VMEM(corner, bf16),
@@ -511,14 +537,14 @@
             pltpu.VMEM(top, bf16),
             dma((6,)),
             dma((6,)),
-            dma((4,)),
+            dma((2,)),
         ]
         + [dma((slots,))] * 4,
         compiler_params=pltpu.CompilerParams(
             collective_id=1, has_side_effects=True, vmem_limit_bytes=VMEM_LIMIT
         ),
         name="give",
-    )(x, w, *pieces)
+    )(w, d_own, x, *pieces)
 
 
 def body(queries, keys, values, projection, d_outputs):
@@ -543,32 +569,8 @@
     for step in range(dp_count):
         owner = lax.rem(dp_index + step, dp_count)
         sliced.append(lax.dynamic_slice_in_dim(attended, owner * depth, depth, 1))
-    own, arrived, from_top, from_bottom, from_left, from_right = give(
-        jnp.stack(sliced), projection, d_pieces
-    )
-
-    def present(array, axis, step):
-        index = lax.axis_index(axis)
-        there = (index - step >= 0) & (index - step < lax.axis_size(axis))
-        return jnp.where(there, array.astype(f32), 0.0)
-
-    summed = d_own + jnp.concatenate(
-        (present(from_left, "tm", 1), present(from_right, "tm", -1)), axis=1
-    )
-    summed = summed + jnp.concatenate(
-        (present(from_top, "height", 1), present(from_bottom, "height", -1)), axis=2
-    )
-    summed = summed.astype(bf16)
-    outputs = own
-    for step in range(1, dp_count):
-        outputs = outputs + arrived[step - 1].astype(f32)
-    outputs = outputs.astype(bf16)
-    return (
-        outputs.reshape(d_outputs.shape),
-        d_queries[None],
-        summed[0][None],
-        summed[1][None],
-    )
+    outputs, d_keys, d_values = give(jnp.stack(sliced), projection, d_own, d_pieces)
+    return (outputs[None], d_queries[None], d_keys[None], d_values[None])
 
 
 def solution(mesh):

time: 122 us -> 126 us (1.033)
  local copies, waits for them, and re-layouts: 4.62 us -> 9.9 us
  other arithmetic: 6.73 us -> 3.3 us
  Pallas kernels: 109 us -> 111 us
    unnamed x18 -> x5, local copies, waits for them, and re-layouts: 1.23 us -> 6.73 us
    select_n x2 -> x0, other arithmetic: 3.2 us -> none  [present(): return jnp.where(there, array.astype(f32), 0.0)]
    pallas_call x1, Pallas kernels: 57.9 us -> 60.2 us  [give(): pl.pallas_call(give_kernel, out_shape=outs, in_specs=[anywhere] * 2 + [in...]
    convert_element_type x2 -> x0, other arithmetic: 1.78 us -> none  [the longest x1 0.95 us: body(): outputs = outputs.astype(bf16)]
where the time goes in v4:
time: 126 us; the launch traced here: 125 us
  Pallas kernels  111 us (88%)
  local copies, waits for them, and re-layouts  9.9 us (8%)
  other arithmetic  3.3 us (3%)
    pallas_call x1, Pallas kernels, give(): pl.pallas_call(give_kernel, out_shape=outs, in_specs=[anywhere] * 2 + [in...  60.2 us
    pallas_call x1, Pallas kernels, fetch(): pl.pallas_call(fetch_kernel, out_shape=[jax.ShapeDtypeStruct(s, bf16) for...  34.1 us
    pallas_call x1, Pallas kernels, attention(): pl.pallas_call(functools.partial(attention_kernel, width // HDIM, 1.0 / m...  17 us
    unnamed x5, local copies, waits for them, and re-layouts  6.73 us

profile of v4, /device:TPU:1, one launch (start us, length us, event | category | flops | bytes accessed | tf_op | source)
XLA Modules:
  0.0 125.2 jit_solution(5234256590603081770)
XLA Ops:
  0.6 0.7 fusion.6
  1.4 1.7 %and_select_fusion.bias_ref = f32[512,128]{1,0:T(8,128)} fusion(pred[512,128]{1,0:T(32,128)(4,1)} %constant.48.clone, pred[512]{0:T(512)(128)(4,1)S(1)} %fusion.6), kind=kLoop, calls=%fused_computation.5 | loop fusion | flops 131072 | bytes 328192 | tf_op jit(solution)/shard_map/jit(_where)/select_n | solution.py:62
  3.1 34.1 %fetch.1 = (bf16[2,4,2,8,2560]{4,3,2,1,0:T(8,128)(2,1)}, bf16[2,4,2,8,2560]{4,3,2,1,0:T(8,128)(2,1)}, bf16[2,2,4,8,2560]{4,3,2,1,0:T(8,128)(2,1)}, bf16[2,2,4,8,...) custom-call(bf16[4,4,8,2560]{3,2,1,0:T(8,128)(2,1)} %bitcast.17, ...), custom_call_target="tpu_custom_call" | custom-call | tf_op jit(solution)/shard_map/fetch/pallas_call | solution.py:361
  37.2 1.0 bitcast_dynamic-update-slice_fusion.1
  38.2 1.0 bitcast_dynamic-update-slice_fusion.da_ref
  39.2 0.0 copy-start
  39.3 0.8 copy-done
  40.1 17.0 %attention.1 = (bf16[128,2560]{1,0:T(8,128)(2,1)}, bf16[4,4,8,2560]{3,2,1,0:T(8,128)(2,1)}, f32[2,4,4,8,2560]{4,3,2,1,0:T(8,128)}, bf16[2,4,2,8,2560]{4,3,2,1,0:...) custom-call(f32[512,128]{1,0:T(8,128)} %and_select_fusion.bias_ref, ...), custom_call_target="tpu_custom_call" | custom-call | flops 2013265920 | bytes 13107200 | tf_op jit(solution)/shard_map/attention/pallas_call | solution.py:160
  57.1 1.1 dynamic-slice_bitcast_fusion.1
  58.2 0.9 pad_maximum_fusion.x_ref
  59.1 60.2 %give.1 = (bf16[4,4,8,2560]{3,2,1,0:T(8,128)(2,1)}, bf16[4,4,8,2560]{3,2,1,0:T(8,128)(2,1)}, bf16[4,4,8,2560]{3,2,1,0:T(8,128)(2,1)}) custom-call(bf16[1280,2560]{1,0:T(8,128)(2,1)} %w_ref.3, f32[2,4,4,8,2560]{4,3,2,1,0:T(8,128)} %get-tuple-element.30.d_own_ref, bf16[2,128,1280]{2,1,0:T(8,128)(2,1)} %pad_maximum_fusion.x_ref, ...), custom_call_target="tpu_custom_call" | custom-call | tf_op jit(solution)/shard_map/give/pallas_call | solution.py:518
  119.3 2.0 %copy.18 = bf16[1,4,4,8,2560]{4,3,2,1,0:T(8,128)(2,1)} copy(bf16[1,4,4,8,2560]{4,3,2,1,0:T(8,128)(2,1)} %bitcast.23) | data formatting | bytes 1310720
  121.3 2.0 %copy.19 = bf16[1,4,4,8,2560]{4,3,2,1,0:T(8,128)(2,1)} copy(bf16[1,4,4,8,2560]{4,3,2,1,0:T(8,128)(2,1)} %bitcast.22) | data formatting | bytes 1310720
  123.2 2.0 %copy.20 = bf16[1,4,4,8,2560]{4,3,2,1,0:T(8,128)(2,1)} copy(bf16[1,4,4,8,2560]{4,3,2,1,0:T(8,128)(2,1)} %bitcast.21) | data formatting | bytes 1310720
  (1 shorter events, 0.0 us)
Async XLA Ops:
  39.2 0.8 copy-start

commit v5 on v4

--- a/solution.py
+++ b/solution.py
@@ -264,6 +264,8 @@
     x_held,
     x_arrived,
     part_held,
+    zeros,
+    corner_zeros,
     send_sem,
     recv_sem,
     local_sem,
@@ -274,6 +276,9 @@
 ):
     dp_count = lax.axis_size("dp")
     half = k_ref.shape[0] // 2
+    zeros[...] = jnp.zeros_like(zeros)
+    corner_zeros[...] = jnp.zeros_like(corner_zeros)
+    no_rows, no_frames = zeros.at[:, :half], zeros.at[:half]
     greet()
     first, filled = [], []
 
@@ -287,8 +292,8 @@
 
     for which, ref in enumerate((k_ref, v_ref)):
         low, high = ref.at[:, :half], ref.at[:, half:]
-        shift(high, top_ref.at[which], high, "height", 1, first)
-        shift(low, bottom_ref.at[which], low, "height", -1, first)
+        shift(high, top_ref.at[which], no_rows, "height", 1, first)
+        shift(low, bottom_ref.at[which], no_rows, "height", -1, first)
     exchange = []
     for step in range(1, dp_count):
         s = step - 1
@@ -297,8 +302,8 @@
         exchange.append(move)
     for which, ref in enumerate((k_ref, v_ref)):
         low, high = ref.at[:half], ref.at[half:]
-        shift(high, left_ref.at[which], high, "tm", 1, first)
-        shift(low, right_ref.at[which], low, "tm", -1, first)
+        shift(high, left_ref.at[which], no_frames, "tm", 1, first)
+        shift(low, right_ref.at[which], no_frames, "tm", -1, first)
     load_w = pltpu.make_async_copy(w_ref, w_held, local_sem.at[12])
     load_x = pltpu.make_async_copy(x_ref, x_held, local_sem.at[13])
     load_x.start()
@@ -334,8 +339,8 @@
         settle(move, fill)
     for side, ref in enumerate((top_ref, bottom_ref)):
         low, high = ref.at[:, :half], ref.at[:, half:]
-        shift(high, corner_left_ref.at[:, side], high, "tm", 1, second)
-        shift(low, corner_right_ref.at[:, side], low, "tm", -1, second)
+        shift(high, corner_left_ref.at[:, side], corner_zeros, "tm", 1, second)
+        shift(low, corner_right_ref.at[:, side], corner_zeros, "tm", -1, second)
     for move, fill in first[4:] + second:
         settle(move, fill)
     for move, _ in first + second:
@@ -368,6 +373,8 @@
             pltpu.VMEM(x.shape, bf16),
             pltpu.VMEM((slots,) + x.shape, bf16),
             pltpu.VMEM((others + 1, count, w.shape[0]), bf16),
+            pltpu.VMEM(k.shape, bf16),
+            pltpu.VMEM((2, half, half, cols, dim), bf16),
             dma((12,)),
             dma((12,)),
             dma((15,)),

time: 126 us -> 93.9 us (0.75)
  Pallas kernels: 111 us -> 79.3 us
    pallas_call x1, Pallas kernels: 60.2 us -> 30.3 us  [give(): pl.pallas_call(give_kernel, out_shape=outs, in_specs=[anywhere] * 2 + [in...]
    pallas_call x1, Pallas kernels: 34.1 us -> 32 us  [fetch(): pl.pallas_call(fetch_kernel, out_shape=[jax.ShapeDtypeStruct(s, bf16) for...]
where the time goes in v5:
time: 93.9 us; the launch traced here: 93.2 us
  Pallas kernels  79.3 us (84%)
  local copies, waits for them, and re-layouts  9.9 us (11%)
  other arithmetic  3.3 us (4%)
    pallas_call x1, Pallas kernels, fetch(): pl.pallas_call(fetch_kernel, out_shape=[jax.ShapeDtypeStruct(s, bf16) for...  32 us
    pallas_call x1, Pallas kernels, give(): pl.pallas_call(give_kernel, out_shape=outs, in_specs=[anywhere] * 2 + [in...  30.3 us
    pallas_call x1, Pallas kernels, attention(): pl.pallas_call(functools.partial(attention_kernel, width // HDIM, 1.0 / m...  17 us
    unnamed x5, local copies, waits for them, and re-layouts  6.73 us
    dynamic_update_slice x2, local copies, waits for them, and re-layouts, body(): lax.dynamic_update_slice_in_dim(d_attended, parts[step], owner * depth, 1)  2 us

profile of v5, /device:TPU:1, one launch (start us, length us, event | category | flops | bytes accessed | tf_op | source)
XLA Modules:
  0.0 93.2 jit_solution(11620735952942336287)
XLA Ops:
  0.6 0.7 fusion.6
  1.4 1.7 %and_select_fusion.bias_ref = f32[512,128]{1,0:T(8,128)} fusion(pred[512,128]{1,0:T(32,128)(4,1)} %constant.48.clone, pred[512]{0:T(512)(128)(4,1)S(1)} %fusion.6), kind=kLoop, calls=%fused_computation.5 | loop fusion | flops 131072 | bytes 328192 | tf_op jit(solution)/shard_map/jit(_where)/select_n | solution.py:62
  3.1 32.0 %fetch.1 = (bf16[2,4,2,8,2560]{4,3,2,1,0:T(8,128)(2,1)}, bf16[2,4,2,8,2560]{4,3,2,1,0:T(8,128)(2,1)}, bf16[2,2,4,8,2560]{4,3,2,1,0:T(8,128)(2,1)}, bf16[2,2,4,8,...) custom-call(bf16[4,4,8,2560]{3,2,1,0:T(8,128)(2,1)} %bitcast.17, ...), custom_call_target="tpu_custom_call" | custom-call | tf_op jit(solution)/shard_map/fetch/pallas_call | solution.py:366
  35.1 1.0 %bitcast_dynamic-update-slice_fusion.1 = bf16[128,2560]{1,0:T(8,128)(2,1)S(1)} fusion(bf16[128,2560]{1,0:T(8,128)(2,1)S(1)} %broadcast_in_dim.27, s32[]{:T(128)S(6)} %select_n.13, bf16[2,128,1280]{2,1,0:T(8,128)(2,1)} %get-tuple-element.29), kind=kLoop, calls=%fused_computation.2 | loop fusion | bytes 655364 | tf_op jit(solution)/shard_map/dynamic_update_slice | solution.py:570
  36.1 1.0 %bitcast_dynamic-update-slice_fusion.da_ref = bf16[128,2560]{1,0:T(8,128)(2,1)S(1)} fusion(bf16[128,2560]{1,0:T(8,128)(2,1)S(1)} %bitcast_dynamic-update-slice_fusion.1, s32[]{:T(128)S(6)} %select_n.14, bf16[2,128,1280]{2,1,0:T(8,128)(2,1)} %get-tuple-element.29), kind=kLoop, calls=%fused_computation.1 | loop fusion | bytes 655364 | tf_op jit(solution)/shard_map/dynamic_update_slice | solution.py:570
  37.1 0.0 copy-start
  37.1 0.8 copy-done
  37.9 17.0 %attention.1 = (bf16[128,2560]{1,0:T(8,128)(2,1)}, bf16[4,4,8,2560]{3,2,1,0:T(8,128)(2,1)}, f32[2,4,4,8,2560]{4,3,2,1,0:T(8,128)}, bf16[2,4,2,8,2560]{4,3,2,1,0:...) custom-call(f32[512,128]{1,0:T(8,128)} %and_select_fusion.bias_ref, ...), custom_call_target="tpu_custom_call" | custom-call | flops 2013265920 | bytes 13107200 | tf_op jit(solution)/shard_map/attention/pallas_call | solution.py:160
  55.0 1.1 %dynamic-slice_bitcast_fusion.1 = (bf16[1,128,1280]{2,1,0:T(8,128)(2,1)S(1)}, bf16[1,128,1280]{2,1,0:T(8,128)(2,1)S(1)}) fusion(bf16[128,2560]{1,0:T(8,128)(2,1)} %get-tuple-element.31, s32[]{:T(128)S(6)} %select_n.13, s32[]{:T(128)S(6)} %select_n.14), kind=kLoop, calls=%fused_computation.4 | loop fusion | bytes 1310728 | tf_op jit(solution)/shard_map/stack | solution.py:579
  56.1 0.9 pad_maximum_fusion.x_ref
  57.0 30.3 %give.1 = (bf16[4,4,8,2560]{3,2,1,0:T(8,128)(2,1)}, bf16[4,4,8,2560]{3,2,1,0:T(8,128)(2,1)}, bf16[4,4,8,2560]{3,2,1,0:T(8,128)(2,1)}) custom-call(bf16[1280,2560]{1,0:T(8,128)(2,1)} %w_ref.3, f32[2,4,4,8,2560]{4,3,2,1,0:T(8,128)} %get-tuple-element.30.d_own_ref, bf16[2,128,1280]{2,1,0:T(8,128)(2,1)} %pad_maximum_fusion.x_ref, ...), custom_call_target="tpu_custom_call" | custom-call | tf_op jit(solution)/shard_map/give/pallas_call | solution.py:525
  87.3 2.0 %copy.18 = bf16[1,4,4,8,2560]{4,3,2,1,0:T(8,128)(2,1)} copy(bf16[1,4,4,8,2560]{4,3,2,1,0:T(8,128)(2,1)} %bitcast.23) | data formatting | bytes 1310720
  89.3 2.0 %copy.19 = bf16[1,4,4,8,2560]{4,3,2,1,0:T(8,128)(2,1)} copy(bf16[1,4,4,8,2560]{4,3,2,1,0:T(8,128)(2,1)} %bitcast.22) | data formatting | bytes 1310720
  91.2 2.0 %copy.20 = bf16[1,4,4,8,2560]{4,3,2,1,0:T(8,128)(2,1)} copy(bf16[1,4,4,8,2560]{4,3,2,1,0:T(8,128)(2,1)} %bitcast.21) | data formatting | bytes 1310720
  (1 shorter events, 0.0 us)
Async XLA Ops:
  37.1 0.8 copy-start
